TPU v7x, 128 devices: a whole 4x4x4 slice. The times are simulated.
128 devices in a mesh: gx: 4 (over z), gy: 4 (over x_lo, core), gz: 8 (over x_hi, y).
Axes of the slice: x: 4 (x_hi: 2, x_lo: 2; x = x_hi * 2 + x_lo), y: 4, z: 4, core: 2. Of those that a mesh axis runs over, the one named last changes fastest.
Arguments:
- charge: float32 [131072, 128], P(('gx', 'gy', 'gz')), may hold values from -4 to 4
- positions: float32 [3, 131072, 128], P(None, ('gx', 'gy', 'gz')), may hold values from 0 to 4
- counts: int32 [131072], P(('gx', 'gy', 'gz')), may hold values from 64 to 128, as said below
- corner: int32 [131072], P(('gx', 'gy', 'gz')), may hold values from 5462 to 81962, as said below
- fine_taps: float32 [2, 23], replicated, may hold values from 0 to 3, as said below
- coarse_taps: float32 [2, 23], replicated, may hold values from 0 to 3, as said below
Outputs:
- atom_potential: float32 [131072, 128], P(('gx', 'gy', 'gz'))
- grid_potential: float32 [128, 128, 512], P('gx', 'gy', 'gz')
Inputs may be any that keep to these rules, and one draw needn't show every extreme that they name: `counts`: every cell holds 64 to 128 atoms; in every draw some cell is full. Each device lists its own cells once each, in some order; the cell with local cell coordinates (a, b, c) has corner ((4a + 2)(38) + 4b + 2)(70) + 4c + 2. `fine_taps`: positive taps. `coarse_taps`: positive taps.
All inputs are finite; a program needn't handle non-finite values.
Results may differ from a plain program's by a relative error of at most 0.0003.
Values sent between devices are 32-bit elements; how exact they have to be, the bound alone decides.
A program may use at most 192 MiB of HBM per device.

v0:
```python
import jax
import jax.numpy as jnp
from jax import lax
from jax.experimental import pallas as pl
from jax.experimental.pallas import tpu as pltpu
from jax.sharding import PartitionSpec as P

CX = 32
CY = 32
CZ = 64
f32 = jnp.float32
bf16 = jnp.bfloat16


def split(v):
    hi = v.astype(bf16)
    return hi, (v - hi.astype(f32)).astype(bf16)


def spline8(u, node):
    m = jnp.abs(u - node)
    t = jnp.maximum(2.0 - m, 0.0)
    v = jnp.maximum(1.0 - m, 0.0)
    return t * t * t - 4.0 * (v * v * v)


def row8(ref, lead, n):
    v = ref[pl.ds(n, 1), :] if lead is None else ref[lead, pl.ds(n, 1), :]
    return jnp.broadcast_to(v, (8, 128))


def spread_kernel(inv_ref, cnt_ref, q_ref, pos_ref, out_ref, acc, lhs, rhs):
    node = lax.broadcasted_iota(jnp.int32, (8, 128), 0).astype(f32) - 1.0
    lane = lax.broadcasted_iota(jnp.int32, (8, 128), 1)
    zero = jnp.zeros((8, 128), f32)
    acc[...] = jnp.zeros_like(acc)
    rhs[...] = jnp.zeros_like(rhs)

    def build(row, slot):
        for cz in range(16):
            n = inv_ref[row * 16 + cz]
            q = row8(q_ref, None, n)
            q = jnp.where(lane < cnt_ref[n], q * (1.0 / 216.0), 0.0)
            qx = q * spline8(row8(pos_ref, 0, n), node)
            wy = spline8(row8(pos_ref, 1, n), node)
            wz = spline8(row8(pos_ref, 2, n), node)
            prod = jnp.concatenate([qx[a : a + 1] * wy for a in range(8)], axis=0)
            hi, lo = split(prod)
            here = slice(cz * 128, cz * 128 + 128)
            lhs[slot, 0:64, here] = hi
            lhs[slot, 64:128, here] = lo
            pair = cz // 2
            base = 64 * (cz % 2) + 16 * (pair // 2)
            tile = jnp.concatenate([zero, wz] if pair % 2 else [wz, zero], axis=0)
            hi, lo = split(tile)
            rhs[slot, base : base + 16, here] = hi
            rhs[slot, 128 + base : 144 + base, here] = lo

    def finish(cx, start, odd, slot):
        r = lax.dot_general(
            lhs[slot], rhs[slot], (((1,), (1,)), ((), ())), preferred_element_type=f32
        )
        s = r[0:64] + r[64:128]
        t = s[:, 0:128] + s[:, 128:256]
        for a in range(8):
            acc[odd, 4 * cx + a, pl.ds(pl.multiple_of(start, 8), 8), :] += t[8 * a : 8 * a + 8]

    build(0, 0)

    def step(i, carry):
        cx = i // 4
        start = (i % 4) * 8
        build(2 * i + 1, 1)
        finish(cx, start, 0, 0)
        build(lax.rem(2 * i + 2, 64), 0)
        finish(cx, start, 1, 1)
        return carry

    lax.fori_loop(0, 32, step, 0)
    lane32 = lax.broadcasted_iota(jnp.int32, (32, 128), 1)
    for x in range(6):
        out_ref[x] = jnp.zeros((40, 128), f32)
    for x in range(42, 54):
        out_ref[x] = jnp.zeros((40, 128), f32)
    for x in range(36):
        joined = []
        for odd in range(2):
            v = acc[odd, x]
            low = jnp.where(lane32 < 64, v, 0.0)
            joined.append(pltpu.roll(low, 11, 1) + pltpu.roll(v - low, 79, 1))
        out_ref[6 + x, 0:32, :] = joined[0]
        out_ref[6 + x, 32:40, :] = jnp.zeros((8, 128), f32)
        out_ref[6 + x, 4:36, :] += joined[1]


SMEM = pl.BlockSpec(memory_space=pltpu.SMEM)
VMEM = pl.BlockSpec(memory_space=pltpu.VMEM)


def spread(inv, counts, charge, positions):
    return pl.pallas_call(
        spread_kernel,
        out_shape=jax.ShapeDtypeStruct((54, 40, 128), f32),
        in_specs=[SMEM, SMEM, VMEM, VMEM],
        out_specs=VMEM,
        scratch_shapes=[
            pltpu.VMEM((2, 36, 32, 128), f32),
            pltpu.VMEM((2, 128, 2048), bf16),
            pltpu.VMEM((2, 256, 2048), bf16),
        ],
        compiler_params=pltpu.CompilerParams(vmem_limit_bytes=48 * 1024 * 1024),
    )(inv, counts, charge, positions)


def sample_kernel(inv_ref, cnt_ref, pos_ref, v_ref, out_ref, grid_ref, vs, rhs):
    node = lax.broadcasted_iota(jnp.int32, (8, 128), 0).astype(f32) - 1.0
    lane = lax.broadcasted_iota(jnp.int32, (1, 128), 1)
    lane40 = lax.broadcasted_iota(jnp.int32, (40, 128), 1)
    zero = jnp.zeros((8, 128), f32)
    rhs[...] = jnp.zeros_like(rhs)
    for x in range(36):
        v = v_ref[x]
        if 1 <= x < 33:
            grid_ref[x - 1] = v[1:33, 0:64]
        v = jnp.where(lane40 < 68, pltpu.roll(v, 1, 1), 0.0) * (1.0 / 216.0)
        hi = v.astype(bf16).astype(f32)
        lo = (v - hi).astype(bf16).astype(f32)
        first = jnp.where(lane40 < 80, hi, pltpu.roll(lo, 80, 1))
        second = jnp.where(lane40 < 32, pltpu.roll(lo, 80, 1), pltpu.roll(hi, 32, 1))
        vs[0, x, :, 0:128] = first[0:32]
        vs[0, x, :, 128:256] = second[0:32]
        vs[1, x, :, 0:128] = first[4:36]
        vs[1, x, :, 128:256] = second[4:36]

    def one(cx, start, odd, row):
        left = vs[odd, pl.ds(4 * cx, 8), pl.ds(pl.multiple_of(start, 8), 8), :]
        left = left.reshape(64, 256).astype(bf16)
        for k in range(8):
            ns, ws = [], []
            for p in range(2):
                n = inv_ref[row * 16 + 2 * k + p]
                wz = spline8(row8(pos_ref, 2, n), node)
                if k % 2 == 0:
                    parts = [wz, zero]
                    if p:
                        parts = [pltpu.roll(jnp.concatenate(parts, 0), 4, 0)]
                else:
                    parts = [zero, wz, zero, zero]
                    if p:
                        parts = [zero, pltpu.roll(jnp.concatenate([wz, zero], 0), 4, 0), zero]
                hi, lo = split(jnp.concatenate(parts, 0))
                base = 16 * (k // 2)
                size = hi.shape[0]
                here = slice(p * 128, p * 128 + 128)
                rhs[odd, k, base : base + size, here] = hi
                rhs[odd, k, 80 + base : 80 + base + size, here] = hi
                rhs[odd, k, 160 + base : 160 + base + size, here] = lo
                ns.append(n)
            f = jnp.dot(left[:, 0:240], rhs[odd, k], preferred_element_type=f32)
            for p in range(2):
                n = ns[p]
                wx = spline8(row8(pos_ref, 0, n), node)
                wy = spline8(row8(pos_ref, 1, n), node)
                here = slice(p * 128, p * 128 + 128)
                g = wx[0:1] * f[0:8, here]
                for a in range(1, 8):
                    g = g + wx[a : a + 1] * f[8 * a : 8 * a + 8, here]
                r = jnp.sum(g * wy, axis=0, keepdims=True)
                out_ref[pl.ds(n, 1), :] = jnp.where(lane < cnt_ref[n], r, 0.0)

    def step(i, carry):
        cx = i // 4
        start = (i % 4) * 8
        one(cx, start, 0, 2 * i)
        one(cx, start, 1, 2 * i + 1)
        return carry

    lax.fori_loop(0, 32, step, 0)


def sample(inv, counts, positions, grid):
    return pl.pallas_call(
        sample_kernel,
        out_shape=(
            jax.ShapeDtypeStruct((1024, 128), f32),
            jax.ShapeDtypeStruct((32, 32, 64), f32),
        ),
        in_specs=[SMEM, SMEM, VMEM, VMEM],
        out_specs=(VMEM, VMEM),
        scratch_shapes=[
            pltpu.VMEM((2, 36, 32, 256), f32),
            pltpu.VMEM((2, 8, 240, 256), bf16),
        ],
        compiler_params=pltpu.CompilerParams(vmem_limit_bytes=48 * 1024 * 1024),
    )(inv, counts, positions, grid)


MESH = pl.DeviceIdType.MESH


def iota(shape, dim):
    return lax.broadcasted_iota(jnp.int32, shape, dim)


def weight_of(gap):
    size = jnp.abs(gap)
    return jnp.where(
        size == 0, 1.0, jnp.where(size == 1, 0.5625, jnp.where(size == 3, -0.0625, 0.0))
    )


def banded(gap, values, reach):
    total = jnp.zeros(gap.shape, f32)
    for m in range(-reach, reach + 1):
        total = total + jnp.where(gap == m, values[m + reach], 0.0)
    return total


def right(v, twice, rest):
    hi, lo = split(v)
    r = jnp.dot(jnp.concatenate([hi, lo], 1), twice, preferred_element_type=f32)
    return r + jnp.dot(hi, rest, preferred_element_type=f32)


def right_exact(v, twice):
    hi, lo = split(v)
    return jnp.dot(jnp.concatenate([hi, lo], 1), twice, preferred_element_type=f32)


def field_kernel(
    ft, ct, q_ref, v_ref,
    zs, zr, a_ref, ys, yr, xr, ext, rs, rr,
    c_ref, cxs, cxr, cext, d_ref, czs, czr, e_ref, cys, cyr, g_ref,
    cz_m, my_m, rz_m, ry_m, ccz_m, cmy_m, pz_m, ssem, rsem,
):
    ids = {name: lax.axis_index(name) for name in ("gx", "gy", "gz")}
    size_of = {"gx": 4, "gy": 4, "gz": 8}

    def away(name, step):
        count = size_of[name]
        return {name: lax.rem(ids[name] + (step + count), count)}

    for s in range(2):
        for j in range(21, 24):
            cyr[s, j] = jnp.zeros((16, 128), f32)
    barrier = pltpu.get_barrier_semaphore()
    for name in ("gx", "gy", "gz"):
        for step in (1, -1):
            pl.semaphore_signal(barrier, inc=1, device_id=away(name, step), device_id_type=MESH)

    lane = iota((1, 128), 1)
    lane40 = iota((40, 128), 1)
    lane24 = iota((24, 128), 1)
    half40 = lane40 % 64
    half24 = lane24 % 64

    def send(stage, name, up_src, up_dst, down_src, down_dst):
        copies = []
        for k, (step, src, dst) in enumerate(((1, up_src, up_dst), (-1, down_src, down_dst))):
            copy = pltpu.make_async_remote_copy(
                src_ref=src,
                dst_ref=dst,
                send_sem=ssem.at[stage, k],
                recv_sem=rsem.at[stage, k],
                device_id=away(name, step),
                device_id_type=MESH,
            )
            copy.start()
            copies.append(copy)
        return copies

    def finish(copies):
        for copy in copies:
            copy.wait()

    def pack_z(g, carry):
        up = jnp.zeros((40, 128), f32)
        down = jnp.zeros((40, 128), f32)
        for i in range(8):
            v = q_ref[6 + 8 * g + i]
            here = lane40 // 16 == i
            up = jnp.where(here, pltpu.roll(v, (16 * i - 64) % 128, 1), up)
            down = jnp.where(here, pltpu.roll(v, (16 * i - 11) % 128, 1), down)
        zs[0, g] = up
        zs[1, g] = down
        return carry

    lax.fori_loop(0, 5, pack_z, 0)
    pl.semaphore_wait(barrier, 6)
    z_copies = send(0, "gz", zs.at[0], zr.at[0], zs.at[1], zr.at[1])

    gap = iota((256, 128), 0) % 128 - 12 - 2 * (iota((256, 128), 1) % 64 - 13)
    node = iota((256, 128), 1) % 64 - 13
    rz_m[...] = jnp.where((node >= -2) & (node <= 34), weight_of(gap), 0.0).astype(bf16)
    gap = iota((24, 96), 1) % 48 - 2 * iota((24, 96), 0) + 3
    ry_m[...] = jnp.where(iota((24, 96), 1) % 48 < 40, weight_of(gap), 0.0).astype(bf16)

    def shrink(g, carry):
        rows = []
        for i in range(4):
            first = 2 * (4 * g + i)
            near = q_ref[first + 2] + q_ref[first + 4]
            wide = q_ref[first] + q_ref[first + 6]
            rows.append(q_ref[first + 3] + 0.5625 * near - 0.0625 * wide)
        r = right_exact(jnp.concatenate(rows, 0), rz_m[...])
        r = jnp.concatenate([r[40 * i : 40 * i + 40] for i in range(4)], 1)
        r = jnp.concatenate([r, jnp.zeros((8, 512), f32)], 0)
        hi, lo = split(r)
        r = jnp.dot(ry_m[...], jnp.concatenate([hi, lo], 0), preferred_element_type=f32)
        for i in range(4):
            c_ref[4 * g + i] = r[:, 128 * i : 128 * i + 128]
        return carry

    lax.fori_loop(0, 6, shrink, 0)
    for k in range(8):
        cxs[0, k] = jnp.where(lane24 < 64, c_ref[5 + k], c_ref[13 + k])
        cxs[1, k] = jnp.where(lane24 < 64, c_ref[k], c_ref[8 + k])
    cx_copies = send(1, "gx", cxs.at[0], cxr.at[0], cxs.at[1], cxr.at[1])

    ftap = [jnp.where(lane < 64, ft[0, m], ft[1, m]) for m in range(23)]
    gap = iota((128, 128), 0) - 12 - iota((128, 128), 1) % 64
    full = banded(gap, ftap, 11)
    hi, lo = split(full)
    cz_m[0:128] = hi
    cz_m[128:256] = hi
    cz_m[256:384] = lo

    def three_parts(rows, width, spots, values, reach):
        col = iota((rows, 256), 1)
        part = col // width
        total = banded(spots(col % width), values, reach)
        hi = total.astype(bf16).astype(f32)
        return jnp.where(part == 2, total - hi, hi).astype(bf16)

    row40 = iota((40, 256), 0)

    def spots_y(col):
        off = jnp.where(col < 40, col, jnp.where(col < 56, col - 52, col - 24))
        return jnp.where(col < 72, off - row40, 99)

    for t in range(2):
        taps = [ft[t, m] for m in range(23)]
        my_m[40 * t : 40 * t + 40] = three_parts(40, 80, spots_y, taps, 11)

    finish(z_copies)

    def conv_z(g, carry):
        up = zr[0, g]
        down = zr[1, g]
        rows = []
        for i in range(8):
            v = q_ref[6 + 8 * g + i]
            v = v + jnp.where(lane40 < 16, pltpu.roll(up, (-16 * i) % 128, 1), 0.0)
            here = (lane40 >= 75) & (lane40 < 91)
            v = v + jnp.where(here, pltpu.roll(down, (75 - 16 * i) % 128, 1), 0.0)
            rows.append(v)
        r = right(jnp.concatenate(rows, 0), cz_m[0:256], cz_m[256:384])
        for i in range(8):
            part = r[40 * i : 40 * i + 40]
            a_ref[8 * g + i] = part
            ys[0, 8 * g + i] = part[20:36]
            ys[1, 8 * g + i] = part[0:16]
        return carry

    lax.fori_loop(0, 5, conv_z, 0)
    own = pl.ds(0, 36)
    y_copies = send(2, "gy", ys.at[0, own], yr.at[0, own], ys.at[1, own], yr.at[1, own])

    ctap = [jnp.where(lane < 64, ct[0, m], ct[1, m]) for m in range(23)]
    gap = iota((128, 128), 0) % 64 - iota((128, 128), 1) % 64 - 11
    gap = jnp.where(iota((128, 128), 0) // 64 == iota((128, 128), 1) // 64, gap, 99)
    hi, lo = split(banded(gap, ctap, 11))
    ccz_m[0:128] = hi
    ccz_m[128:256] = hi
    ccz_m[256:384] = lo
    finish(cx_copies)
    for k in range(21):
        cext[11 + k] = c_ref[k]
    for s in range(2):
        base = 0 if s == 0 else 27
        for k in range(8):
            v = cxr[s, k]
            w = pltpu.roll(v, 64, 1)
            first = jnp.where(lane24 < 64, v, w)
            second = jnp.where(lane24 < 64, w, v)
            if s == 0:
                cext[k] = first
                if 8 + k >= 11:
                    cext[8 + k] += second
                else:
                    cext[8 + k] = second
            else:
                if 27 + k < 32:
                    cext[27 + k] += first
                else:
                    cext[27 + k] = first
                cext[35 + k] = second

    def conv_cx(c, carry):
        rows = pl.ds(pl.multiple_of(8 * c, 8), 8)
        for first in (0, 7, 14):
            acc = ctap[0] * cext[first : first + 7, rows, :]
            for m in range(1, 23):
                acc = acc + ctap[m] * cext[first + m : first + m + 7, rows, :]
            d_ref[first : first + 7, rows, :] = acc
        return carry

    lax.fori_loop(0, 3, conv_cx, 0)
    for j in range(21, 24):
        d_ref[j] = jnp.zeros((24, 128), f32)

    def pack_cz(g, carry):
        up = jnp.zeros((24, 128), f32)
        down = jnp.zeros((24, 128), f32)
        for i in range(4):
            v = d_ref[4 * g + i]
            here = half24 // 16 == i
            up = jnp.where(here, pltpu.roll(v, (16 * i - 32) % 128, 1), up)
            down = jnp.where(here, pltpu.roll(v, (16 * i - 11) % 128, 1), down)
        czs[0, g] = up
        czs[1, g] = down
        return carry

    lax.fori_loop(0, 6, pack_cz, 0)
    cz_copies = send(3, "gz", czs.at[0], czr.at[0], czs.at[1], czr.at[1])

    finish(y_copies)

    def conv_y(h, carry):
        both = []
        for p in range(2):
            x = 2 * h + p
            rows = [a_ref[x], yr[0, x], yr[1, x], jnp.zeros((8, 128), f32)]
            both.append(jnp.concatenate(rows, 0))
        hi, lo = split(jnp.concatenate(both, 1))
        stack = jnp.concatenate([hi, lo, hi], 0)
        r = jnp.dot(my_m[:, 0:240], stack, preferred_element_type=f32)
        for p in range(2):
            part = r[:, 128 * p : 128 * p + 128]
            ext[11 + 2 * h + p] = jnp.where(lane40 < 64, part[0:40], part[40:80])
        return carry

    lax.fori_loop(0, 18, conv_y, 0, unroll=3)
    x_copies = send(
        4, "gx", ext.at[pl.ds(32, 15)], xr.at[0], ext.at[pl.ds(11, 15)], xr.at[1]
    )

    finish(cz_copies)

    def conv_cz(g, carry):
        up = czr[0, g]
        down = czr[1, g]
        rows = []
        for i in range(4):
            v = d_ref[4 * g + i]
            v = v + jnp.where(half24 < 16, pltpu.roll(up, (-16 * i) % 128, 1), 0.0)
            here = (half24 >= 43) & (half24 < 59)
            v = v + jnp.where(here, pltpu.roll(down, (43 - 16 * i) % 128, 1), 0.0)
            rows.append(v)
        r = right(jnp.concatenate(rows, 0), ccz_m[0:256], ccz_m[256:384])
        for i in range(4):
            part = r[24 * i : 24 * i + 24]
            e_ref[4 * g + i] = part
            cys[0, 4 * g + i] = part[5:21]
            cys[1, 4 * g + i] = part[0:16]
        return carry

    lax.fori_loop(0, 6, conv_cz, 0)
    own = pl.ds(0, 21)
    cy_copies = send(5, "gy", cys.at[0, own], cyr.at[0, own], cys.at[1, own], cyr.at[1, own])

    def spots_cy(col):
        spot = jnp.where(col < 24, col - 2, jnp.where(col < 40, col - 37, col - 26))
        valid = ((col < 21) | (col >= 24)) & (col < 56)
        return jnp.where(valid, 2 * spot - (row40 - 1), 99)

    for t in range(2):
        taps = []
        for d in range(-25, 26):
            total = 0.0
            for g, weight in ((0, 1.0), (1, 0.5625), (-1, 0.5625), (3, -0.0625), (-3, -0.0625)):
                if (d + g) % 2 == 0 and abs((d + g) // 2) <= 11:
                    total = total + weight * ct[t, (d + g) // 2 + 11]
            taps.append(total)
        cmy_m[40 * t : 40 * t + 40] = three_parts(40, 64, spots_cy, taps, 25)
    spot = iota((256, 128), 0) % 64 - 2
    point = iota((256, 128), 1)
    point = jnp.where(point == 127, -1, point)
    good = (spot <= 34) & (point <= 66)
    pz_m[...] = jnp.where(good, weight_of(point - 2 * spot), 0.0).astype(bf16)

    finish(x_copies)
    ext[0:11] = xr[0, 0:11]
    ext[11:15] += xr[0, 11:15]
    ext[43:47] += xr[1, 0:4]
    ext[47:58] = xr[1, 4:15]

    def conv_x(k, carry):
        rows = pl.ds(pl.multiple_of(8 * (k // 3), 8), 8)
        first = 12 * lax.rem(k, 3)
        acc = ftap[0] * ext[pl.ds(first, 12), rows, :]
        for m in range(1, 23):
            acc = acc + ftap[m] * ext[pl.ds(first + m, 12), rows, :]
        for i in range(12):
            part = acc[i]
            v_ref[first + i, rows, :] = part + pltpu.roll(part, 64, 1)
        return carry

    lax.fori_loop(0, 15, conv_x, 0)
    for g in range(2):
        up = jnp.zeros((40, 128), f32)
        down = jnp.zeros((40, 128), f32)
        for i in range(32 if g == 0 else 4):
            v = v_ref[32 * g + i]
            here = lane40 // 4 == i
            up = jnp.where(here, pltpu.roll(v, (4 * i - 60) % 128, 1), up)
            down = jnp.where(here, pltpu.roll(v, (4 * i) % 128, 1), down)
        rs[0, g] = up
        rs[1, g] = down
    r_copies = send(6, "gz", rs.at[0], rr.at[0], rs.at[1], rr.at[1])

    finish(cy_copies)

    def conv_cy(h, carry):
        both = []
        for p in range(2):
            j = 2 * h + p
            rows = [e_ref[j], cyr[0, j], cyr[1, j], jnp.zeros((8, 128), f32)]
            both.append(jnp.concatenate(rows, 0))
        hi, lo = split(jnp.concatenate(both, 1))
        stack = jnp.concatenate([hi, lo, hi], 0)
        r = jnp.dot(cmy_m[:, 0:192], stack, preferred_element_type=f32)
        parts = []
        for p in range(2):
            part = r[:, 128 * p : 128 * p + 128]
            parts.append(jnp.where(lane40 < 64, part[0:40], part[40:80]))
        r = right_exact(jnp.concatenate(parts, 0), pz_m[...])
        g_ref[2 * h] = r[0:40]
        g_ref[2 * h + 1] = r[40:80]
        return carry

    lax.fori_loop(0, 11, conv_cy, 0)
    finish(r_copies)
    for x in range(36):
        g, i = x // 32, x % 32
        h = x // 2
        if x % 2:
            far = g_ref[h + 2]
        else:
            far = 0.5625 * (g_ref[h + 1] + g_ref[h + 2]) - 0.0625 * (g_ref[h] + g_ref[h + 3])
        near = jnp.where(lane40 < 64, v_ref[x], 0.0)
        above = pltpu.roll(rr[1, g], (64 - 4 * i) % 128, 1)
        below = pltpu.roll(rr[0, g], (124 - 4 * i) % 128, 1)
        near = jnp.where((lane40 >= 64) & (lane40 < 67), above, near)
        near = jnp.where(lane40 == 127, below, near)
        v_ref[x] = near + far


def field(fine_taps, coarse_taps, grid):
    def scratch(*shape):
        return pltpu.VMEM(shape, f32)

    return pl.pallas_call(
        field_kernel,
        out_shape=jax.ShapeDtypeStruct((36, 40, 128), f32),
        in_specs=[SMEM, SMEM, VMEM],
        out_specs=VMEM,
        scratch_shapes=[
            scratch(2, 5, 40, 128),
            scratch(2, 5, 40, 128),
            scratch(40, 40, 128),
            scratch(2, 40, 16, 128),
            scratch(2, 40, 16, 128),
            scratch(2, 15, 40, 128),
            scratch(58, 40, 128),
            scratch(2, 2, 40, 128),
            scratch(2, 2, 40, 128),
            scratch(24, 24, 128),
            scratch(2, 8, 24, 128),
            scratch(2, 8, 24, 128),
            scratch(43, 24, 128),
            scratch(24, 24, 128),
            scratch(2, 6, 24, 128),
            scratch(2, 6, 24, 128),
            scratch(24, 24, 128),
            scratch(2, 24, 16, 128),
            scratch(2, 24, 16, 128),
            scratch(22, 40, 128),
            pltpu.VMEM((384, 128), bf16),
            pltpu.VMEM((80, 256), bf16),
            pltpu.VMEM((256, 128), bf16),
            pltpu.VMEM((24, 96), bf16),
            pltpu.VMEM((384, 128), bf16),
            pltpu.VMEM((80, 256), bf16),
            pltpu.VMEM((256, 128), bf16),
            pltpu.SemaphoreType.DMA((7, 2)),
            pltpu.SemaphoreType.DMA((7, 2)),
        ],
        compiler_params=pltpu.CompilerParams(
            collective_id=0, has_side_effects=True, vmem_limit_bytes=48 * 1024 * 1024
        ),
    )(fine_taps, coarse_taps, grid)


def body(charge, positions, counts, corner, fine_taps, coarse_taps):
    ext_y = CY + 6
    ext_z = CZ + 6
    cell_x = (corner // (ext_y * ext_z) - 2) // 4
    cell_y = (corner // ext_z % ext_y - 2) // 4
    cell_z = (corner % ext_z - 2) // 4
    lattice = (cell_x * (CY // 4) + cell_y) * (CZ // 4) + cell_z
    spots = jnp.arange(lattice.shape[0])
    inv = jnp.sum(jnp.where(lattice[None, :] == spots[:, None], spots[None, :], 0), axis=1)
    inv = inv.astype(jnp.int32)
    grid = spread(inv, counts, charge, positions)
    values = field(fine_taps, coarse_taps, grid)
    return sample(inv, counts, positions, values)


def solution(mesh):
    placed = (
        P(("gx", "gy", "gz"), None),
        P(None, ("gx", "gy", "gz"), None),
        P(("gx", "gy", "gz")),
        P(("gx", "gy", "gz")),
        P(),
        P(),
    )
    return jax.shard_map(
        body,
        mesh=mesh,
        in_specs=placed,
        out_specs=(P(("gx", "gy", "gz"), None), P("gx", "gy", "gz")),
        check_vma=False,
    )
```

profile of v0, /device:TPU:0, one launch (start us, length us, event | category | flops | bytes accessed | tf_op | source)
XLA Modules:
  0.0 94.1 jit_solution(16456606850205931512)
XLA Ops:
  0.6 0.7 fusion.5
  1.4 0.5 select_reduce_fusion.inv_ref
  1.9 0.0 copy-start
  1.9 1.4 %copy-done = f32[3,1024,128]{2,1,0:T(8,128)S(1)} copy-done((f32[3,1024,128]{2,1,0:T(8,128)S(1)}, f32[3,1024,128]{2,1,0:T(8,128)}, u32[]{:S(2)}) %copy-start) | copy-done | bytes 1572888
  3.3 0.0 copy-start.2
  3.3 1.0 %copy-done.2 = f32[1024,128]{1,0:T(8,128)S(1)} copy-done((f32[1024,128]{1,0:T(8,128)S(1)}, f32[1024,128]{1,0:T(8,128)}, u32[]{:S(2)}) %copy-start.2) | copy-done | bytes 524312
  4.3 0.0 copy-start.3
  4.3 0.7 copy-done.3
  5.0 0.0 copy-start.4
  5.0 0.0 copy-start.5
  5.0 27.0 %shard_map.77.q_ref = f32[54,40,128]{2,1,0:T(8,128)S(1)} custom-call(s32[1024]{0:T(1024)S(1)} %select_reduce_fusion.inv_ref, s32[1024]{0:T(1024)S(1)} %copy-done.3, f32[1024,128]{1,0:T(8,128)S(1)} %copy-done.2, f32[3,1024,128]{2,1,0:T(8,128)S(1)} %copy-done), custom_call_target="tpu_custom_call" | custom-call | tf_op jit(solution)/shard_map/pallas_call | solution.py:101
  32.0 0.0 copy-done.4
  32.0 0.0 copy-done.5
  32.0 0.0 copy-start.1
  32.0 40.7 %shard_map.78.v_ref = f32[36,40,128]{2,1,0:T(8,128)S(1)} custom-call(f32[2,23]{1,0:T(2,128)S(1)} %copy-done.4, f32[2,23]{1,0:T(2,128)S(1)} %copy-done.5, f32[54,40,128]{2,1,0:T(8,128)S(1)} %shard_map.77.q_ref), custom_call_target="tpu_custom_call" | custom-call | tf_op jit(solution)/shard_map/pallas_call | solution.py:563
  72.7 0.0 copy-done.1
  72.7 21.4 %shard_map.79 = (f32[1024,128]{1,0:T(8,128)}, f32[32,32,64]{2,1,0:T(8,128)}) custom-call(s32[1024]{0:T(1024)S(1)} %select_reduce_fusion.inv_ref, s32[1024]{0:T(1024)S(1)} %copy-done.3, f32[3,1024,128]{2,1,0:T(8,128)S(1)} %copy-done.1, f32[36,40,128]{2,1,0:T(8,128)S(1)} %shard_map.78.v_ref), custom_call_target="tpu_custom_call" | custom-call | tf_op jit(solution)/shard_map/pallas_call | solution.py:182
Async XLA Ops:
  1.9 1.4 %copy-start = (f32[3,1024,128]{2,1,0:T(8,128)S(1)}, f32[3,1024,128]{2,1,0:T(8,128)}, u32[]{:S(2)}) copy-start(f32[3,1024,128]{2,1,0:T(8,128)} %pos_ref.3) | copy-start | bytes 4718596
  3.3 1.0 %copy-start.2 = (f32[1024,128]{1,0:T(8,128)S(1)}, f32[1024,128]{1,0:T(8,128)}, u32[]{:S(2)}) copy-start(f32[1024,128]{1,0:T(8,128)} %q_ref.1) | copy-start | bytes 1572868
  4.3 0.7 copy-start.3
  5.0 27.0 %copy-start.4 = (f32[2,23]{1,0:T(2,128)S(1)}, f32[2,23]{1,0:T(2,128)}, u32[]{:S(2)}) copy-start(f32[2,23]{1,0:T(2,128)} %ft.1) | copy-start | bytes 556
  5.0 27.0 %copy-start.5 = (f32[2,23]{1,0:T(2,128)S(1)}, f32[2,23]{1,0:T(2,128)}, u32[]{:S(2)}) copy-start(f32[2,23]{1,0:T(2,128)} %ct.1) | copy-start | bytes 556
  32.0 40.7 %copy-start.1 = (f32[3,1024,128]{2,1,0:T(8,128)S(1)}, f32[3,1024,128]{2,1,0:T(8,128)}, u32[]{:S(2)}) copy-start(f32[3,1024,128]{2,1,0:T(8,128)} %pos_ref.3) | copy-start | bytes 4718596
where the time goes:
time: 95.2 us; the launch traced here: 94.1 us
  Pallas kernels  89 us (93%)
  local copies, waits for them, and re-layouts  3.14 us (3%)
  other arithmetic  1.23 us (1%)
    pallas_call x1, Pallas kernels, field(): pl.pallas_call(field_kernel, out_shape=jax.ShapeDtypeStruct((36, 40, 128)...  40.7 us
    pallas_call x1, Pallas kernels, spread(): pl.pallas_call(spread_kernel, out_shape=jax.ShapeDtypeStruct((54, 40, 128...  27 us
    pallas_call x1, Pallas kernels, sample(): pl.pallas_call(sample_kernel, out_shape=(jax.ShapeDtypeStruct((1024, 128)...  21.4 us
    unnamed x12, local copies, waits for them, and re-layouts  3.14 us

commit v1 on v0

--- a/solution.py
+++ b/solution.py
@@ -1,5 +1,6 @@
 import jax
 import jax.numpy as jnp
+import numpy as np
 from jax import lax
 from jax.experimental import pallas as pl
 from jax.experimental.pallas import tpu as pltpu
@@ -29,68 +30,94 @@
     return jnp.broadcast_to(v, (8, 128))
 
 
-def spread_kernel(inv_ref, cnt_ref, q_ref, pos_ref, out_ref, acc, lhs, rhs):
+def row8_at(ref, at, a):
+    return jnp.broadcast_to(ref[at, 0, a : a + 1, :], (8, 128))
+
+
+def spread_kernel(inv_ref, cnt_ref, q_ref, pos_ref, out_ref, xy_ref, z_ref, acc, place, qs, ts):
     node = lax.broadcasted_iota(jnp.int32, (8, 128), 0).astype(f32) - 1.0
     lane = lax.broadcasted_iota(jnp.int32, (8, 128), 1)
     zero = jnp.zeros((8, 128), f32)
     acc[...] = jnp.zeros_like(acc)
-    rhs[...] = jnp.zeros_like(rhs)
-
-    def build(row, slot):
-        for cz in range(16):
-            n = inv_ref[row * 16 + cz]
-            q = row8(q_ref, None, n)
-            q = jnp.where(lane < cnt_ref[n], q * (1.0 / 216.0), 0.0)
-            qx = q * spline8(row8(pos_ref, 0, n), node)
-            wy = spline8(row8(pos_ref, 1, n), node)
-            wz = spline8(row8(pos_ref, 2, n), node)
-            prod = jnp.concatenate([qx[a : a + 1] * wy for a in range(8)], axis=0)
-            hi, lo = split(prod)
-            here = slice(cz * 128, cz * 128 + 128)
-            lhs[slot, 0:64, here] = hi
-            lhs[slot, 64:128, here] = lo
-            pair = cz // 2
-            base = 64 * (cz % 2) + 16 * (pair // 2)
-            tile = jnp.concatenate([zero, wz] if pair % 2 else [wz, zero], axis=0)
-            hi, lo = split(tile)
-            rhs[slot, base : base + 16, here] = hi
-            rhs[slot, 128 + base : 144 + base, here] = lo
-
-    def finish(cx, start, odd, slot):
-        r = lax.dot_general(
-            lhs[slot], rhs[slot], (((1,), (1,)), ((), ())), preferred_element_type=f32
-        )
-        s = r[0:64] + r[64:128]
-        t = s[:, 0:128] + s[:, 128:256]
+    ts[...] = jnp.zeros_like(ts)
+
+    def cell(row, cz, spot):
+        at = row * 16 + cz
+        n = inv_ref[at]
+        q = jnp.where(lane < cnt_ref[at], row8(q_ref, None, n), 0.0)
+        wx = spline8(row8(pos_ref, 0, n), node)
+        wy = spline8(row8(pos_ref, 1, n), node)
+        wz = spline8(row8(pos_ref, 2, n), node)
+        xy_ref[at, 0] = wx
+        xy_ref[at, 1] = wy
+        qs[spot] = q * wx
+        prod = jnp.concatenate([row8(qs, spot, a) * wy for a in range(8)], axis=0)
+        tile = jnp.concatenate([zero, wz] if cz % 2 else [wz, zero], axis=0)
+        hi, lo = split(tile)
+        z_ref[at, 0] = hi
+        z_ref[at, 1] = lo
+        return split(prod), (hi, lo)
+
+    def line(odd, row):
+        parts = []
+        for half in range(2):
+            for k in range(4):
+                (ah, al), (bh, bl) = cell(row, 8 * half + 2 * k, 16 * odd + 8 * half + 2 * k)
+                (ch, cl), (dh, dl) = cell(row, 8 * half + 2 * k + 1, 16 * odd + 8 * half + 2 * k + 1)
+                left = jnp.concatenate(
+                    [jnp.concatenate([ah, ch], 1), jnp.concatenate([al, cl], 1)], 0
+                )
+                down = jnp.concatenate(
+                    [jnp.concatenate([bh, dh], 1), jnp.concatenate([bl, dl], 1)], 0
+                )
+                r = lax.dot_general(
+                    down, left, (((1,), (1,)), ((), ())), preferred_element_type=f32
+                )
+                parts.append(r[0:16] + r[16:32])
+        ts[odd] = jnp.concatenate(parts, 0)
+
+    def finish(i, odd):
+        spot = pl.ds(pl.multiple_of(i % 4 * 8, 8), 8)
+        t = ts[odd].T
+        t = t[0:64] + t[64:128]
         for a in range(8):
-            acc[odd, 4 * cx + a, pl.ds(pl.multiple_of(start, 8), 8), :] += t[8 * a : 8 * a + 8]
-
-    build(0, 0)
+            acc[odd, 4 * (i // 4) + a, spot, :] += t[8 * a : 8 * a + 8]
 
     def step(i, carry):
-        cx = i // 4
-        start = (i % 4) * 8
-        build(2 * i + 1, 1)
-        finish(cx, start, 0, 0)
-        build(lax.rem(2 * i + 2, 64), 0)
-        finish(cx, start, 1, 1)
+        before = jnp.maximum(i - 1, 0)
+        finish(before, 0)
+        finish(before, 1)
+        line(0, 2 * i)
+        line(1, 2 * i + 1)
         return carry
 
     lax.fori_loop(0, 32, step, 0)
-    lane32 = lax.broadcasted_iota(jnp.int32, (32, 128), 1)
+    finish(31, 0)
+    finish(31, 1)
+
+    lin = lax.broadcasted_iota(jnp.int32, (256, 128), 0) % 128
+    z = 4 * (lin // 8) + lin % 8 + 11
+    place[...] = jnp.where(z == lax.broadcasted_iota(jnp.int32, (256, 128), 1), 1.0, 0.0).astype(bf16)
     for x in range(6):
         out_ref[x] = jnp.zeros((40, 128), f32)
     for x in range(42, 54):
         out_ref[x] = jnp.zeros((40, 128), f32)
-    for x in range(36):
+
+    def close(g, carry):
         joined = []
-        for odd in range(2):
-            v = acc[odd, x]
-            low = jnp.where(lane32 < 64, v, 0.0)
-            joined.append(pltpu.roll(low, 11, 1) + pltpu.roll(v - low, 79, 1))
-        out_ref[6 + x, 0:32, :] = joined[0]
-        out_ref[6 + x, 32:40, :] = jnp.zeros((8, 128), f32)
-        out_ref[6 + x, 4:36, :] += joined[1]
+        for i in range(4):
+            x = 4 * g + i
+            pad = jnp.zeros((4, 128), f32)
+            even = jnp.concatenate([acc[0, x], pad, pad], 0)
+            odd = jnp.concatenate([pad, acc[1, x], pad], 0)
+            joined.append(even + odd)
+        hi, lo = split(jnp.concatenate(joined, 0))
+        r = jnp.dot(jnp.concatenate([hi, lo], 1), place[...], preferred_element_type=f32)
+        for i in range(4):
+            out_ref[6 + 4 * g + i] = r[40 * i : 40 * i + 40] * (1.0 / 216.0)
+        return carry
+
+    lax.fori_loop(0, 9, close, 0)
 
 
 SMEM = pl.BlockSpec(memory_space=pltpu.SMEM)
@@ -100,73 +127,69 @@
 def spread(inv, counts, charge, positions):
     return pl.pallas_call(
         spread_kernel,
-        out_shape=jax.ShapeDtypeStruct((54, 40, 128), f32),
+        out_shape=(
+            jax.ShapeDtypeStruct((54, 40, 128), f32),
+            jax.ShapeDtypeStruct((1024, 2, 8, 128), f32),
+            jax.ShapeDtypeStruct((1024, 2, 16, 128), bf16),
+        ),
         in_specs=[SMEM, SMEM, VMEM, VMEM],
-        out_specs=VMEM,
+        out_specs=(VMEM, VMEM, VMEM),
         scratch_shapes=[
             pltpu.VMEM((2, 36, 32, 128), f32),
-            pltpu.VMEM((2, 128, 2048), bf16),
-            pltpu.VMEM((2, 256, 2048), bf16),
+            pltpu.VMEM((256, 128), bf16),
+            pltpu.VMEM((32, 8, 128), f32),
+            pltpu.VMEM((2, 128, 128), f32),
         ],
-        compiler_params=pltpu.CompilerParams(vmem_limit_bytes=48 * 1024 * 1024),
+        compiler_params=pltpu.CompilerParams(vmem_limit_bytes=28 * 1024 * 1024),
     )(inv, counts, charge, positions)
 
 
-def sample_kernel(inv_ref, cnt_ref, pos_ref, v_ref, out_ref, grid_ref, vs, rhs):
-    node = lax.broadcasted_iota(jnp.int32, (8, 128), 0).astype(f32) - 1.0
+def sample_kernel(inv_ref, cnt_ref, xy_ref, z_ref, v_ref, out_ref, grid_ref, vs, place):
     lane = lax.broadcasted_iota(jnp.int32, (1, 128), 1)
-    lane40 = lax.broadcasted_iota(jnp.int32, (40, 128), 1)
-    zero = jnp.zeros((8, 128), f32)
-    rhs[...] = jnp.zeros_like(rhs)
-    for x in range(36):
-        v = v_ref[x]
-        if 1 <= x < 33:
-            grid_ref[x - 1] = v[1:33, 0:64]
-        v = jnp.where(lane40 < 68, pltpu.roll(v, 1, 1), 0.0) * (1.0 / 216.0)
-        hi = v.astype(bf16).astype(f32)
-        lo = (v - hi).astype(bf16).astype(f32)
-        first = jnp.where(lane40 < 80, hi, pltpu.roll(lo, 80, 1))
-        second = jnp.where(lane40 < 32, pltpu.roll(lo, 80, 1), pltpu.roll(hi, 32, 1))
-        vs[0, x, :, 0:128] = first[0:32]
-        vs[0, x, :, 128:256] = second[0:32]
-        vs[1, x, :, 0:128] = first[4:36]
-        vs[1, x, :, 128:256] = second[4:36]
+
+    lin = lax.broadcasted_iota(jnp.int32, (256, 1024), 0)
+    out = lax.broadcasted_iota(jnp.int32, (256, 1024), 1)
+    within = out % 128
+    z = (8 * (out // 128) + 4 * (within // 8 % 2) + within % 8 - 1) % 128
+    part = within // 16
+    hit = (z == lin % 128) & (part < 3) & ((part == 1) == (lin >= 128))
+    place[...] = jnp.where(hit, 1.0, 0.0).astype(bf16)
+
+    def open_rows(g, carry):
+        rows = []
+        for i in range(4):
+            rows.append(v_ref[4 * g + i])
+        hi, lo = split(jnp.concatenate(rows, 0) * (1.0 / 216.0))
+        both = jnp.concatenate([hi, lo], 1)
+        for k in range(0, 8, 2):
+            r = jnp.dot(both, place[:, 128 * k : 128 * k + 256], preferred_element_type=f32)
+            for i in range(4):
+                for p in range(2):
+                    here = r[40 * i : 40 * i + 40, 128 * p : 128 * p + 128]
+                    vs[0, k + p, 4 * g + i] = here[0:32]
+                    vs[1, k + p, 4 * g + i] = here[4:36]
+        return carry
+
+    lax.fori_loop(0, 9, open_rows, 0)
+    for x in range(32):
+        grid_ref[x] = v_ref[x + 1, 1:33, 0:64]
 
     def one(cx, start, odd, row):
-        left = vs[odd, pl.ds(4 * cx, 8), pl.ds(pl.multiple_of(start, 8), 8), :]
-        left = left.reshape(64, 256).astype(bf16)
         for k in range(8):
-            ns, ws = [], []
+            spot = pl.ds(pl.multiple_of(start, 8), 8)
+            left = vs[odd, k, pl.ds(4 * cx, 8), spot, :].reshape(64, 128).astype(bf16)
+            at = row * 16 + 2 * k
+            hi = jnp.concatenate([z_ref[at, 0], z_ref[at + 1, 0]], 1)
+            lo = jnp.concatenate([z_ref[at, 1], z_ref[at + 1, 1]], 1)
+            right_side = jnp.concatenate([hi, hi, lo], 0)
+            f = jnp.dot(left[:, 0:48], right_side, preferred_element_type=f32)
             for p in range(2):
-                n = inv_ref[row * 16 + 2 * k + p]
-                wz = spline8(row8(pos_ref, 2, n), node)
-                if k % 2 == 0:
-                    parts = [wz, zero]
-                    if p:
-                        parts = [pltpu.roll(jnp.concatenate(parts, 0), 4, 0)]
-                else:
-                    parts = [zero, wz, zero, zero]
-                    if p:
-                        parts = [zero, pltpu.roll(jnp.concatenate([wz, zero], 0), 4, 0), zero]
-                hi, lo = split(jnp.concatenate(parts, 0))
-                base = 16 * (k // 2)
-                size = hi.shape[0]
                 here = slice(p * 128, p * 128 + 128)
-                rhs[odd, k, base : base + size, here] = hi
-                rhs[odd, k, 80 + base : 80 + base + size, here] = hi
-                rhs[odd, k, 160 + base : 160 + base + size, here] = lo
-                ns.append(n)
-            f = jnp.dot(left[:, 0:240], rhs[odd, k], preferred_element_type=f32)
-            for p in range(2):
-                n = ns[p]
-                wx = spline8(row8(pos_ref, 0, n), node)
-                wy = spline8(row8(pos_ref, 1, n), node)
-                here = slice(p * 128, p * 128 + 128)
-                g = wx[0:1] * f[0:8, here]
+                g = row8_at(xy_ref, at + p, 0) * f[0:8, here]
                 for a in range(1, 8):
-                    g = g + wx[a : a + 1] * f[8 * a : 8 * a + 8, here]
-                r = jnp.sum(g * wy, axis=0, keepdims=True)
-                out_ref[pl.ds(n, 1), :] = jnp.where(lane < cnt_ref[n], r, 0.0)
+                    g = g + row8_at(xy_ref, at + p, a) * f[8 * a : 8 * a + 8, here]
+                r = jnp.sum(g * xy_ref[at + p, 1], axis=0, keepdims=True)
+                out_ref[pl.ds(inv_ref[at + p], 1), :] = jnp.where(lane < cnt_ref[at + p], r, 0.0)
 
     def step(i, carry):
         cx = i // 4
@@ -178,21 +201,21 @@
     lax.fori_loop(0, 32, step, 0)
 
 
-def sample(inv, counts, positions, grid):
+def sample(inv, counts, planes, depths, grid):
     return pl.pallas_call(
         sample_kernel,
         out_shape=(
             jax.ShapeDtypeStruct((1024, 128), f32),
             jax.ShapeDtypeStruct((32, 32, 64), f32),
         ),
-        in_specs=[SMEM, SMEM, VMEM, VMEM],
+        in_specs=[SMEM, SMEM, VMEM, VMEM, VMEM],
         out_specs=(VMEM, VMEM),
         scratch_shapes=[
-            pltpu.VMEM((2, 36, 32, 256), f32),
-            pltpu.VMEM((2, 8, 240, 256), bf16),
+            pltpu.VMEM((2, 8, 36, 32, 128), f32),
+            pltpu.VMEM((256, 1024), bf16),
         ],
-        compiler_params=pltpu.CompilerParams(vmem_limit_bytes=48 * 1024 * 1024),
-    )(inv, counts, positions, grid)
+        compiler_params=pltpu.CompilerParams(vmem_limit_bytes=32 * 1024 * 1024),
+    )(inv, counts, planes, depths, grid)
 
 
 MESH = pl.DeviceIdType.MESH
@@ -228,7 +251,7 @@
 
 
 def field_kernel(
-    ft, ct, q_ref, v_ref,
+    taps_ref, q_ref, v_ref,
     zs, zr, a_ref, ys, yr, xr, ext, rs, rr,
     c_ref, cxs, cxr, cext, d_ref, czs, czr, e_ref, cys, cyr, g_ref,
     cz_m, my_m, rz_m, ry_m, ccz_m, cmy_m, pz_m, ssem, rsem,
@@ -317,7 +340,7 @@
         cxs[1, k] = jnp.where(lane24 < 64, c_ref[k], c_ref[8 + k])
     cx_copies = send(1, "gx", cxs.at[0], cxr.at[0], cxs.at[1], cxr.at[1])
 
-    ftap = [jnp.where(lane < 64, ft[0, m], ft[1, m]) for m in range(23)]
+    ftap = [jnp.where(lane < 64, taps_ref[0, m], taps_ref[1, m]) for m in range(23)]
     gap = iota((128, 128), 0) - 12 - iota((128, 128), 1) % 64
     full = banded(gap, ftap, 11)
     hi, lo = split(full)
@@ -339,7 +362,7 @@
         return jnp.where(col < 72, off - row40, 99)
 
     for t in range(2):
-        taps = [ft[t, m] for m in range(23)]
+        taps = [taps_ref[t, m] for m in range(23)]
         my_m[40 * t : 40 * t + 40] = three_parts(40, 80, spots_y, taps, 11)
 
     finish(z_copies)
@@ -366,7 +389,7 @@
     own = pl.ds(0, 36)
     y_copies = send(2, "gy", ys.at[0, own], yr.at[0, own], ys.at[1, own], yr.at[1, own])
 
-    ctap = [jnp.where(lane < 64, ct[0, m], ct[1, m]) for m in range(23)]
+    ctap = [jnp.where(lane < 64, taps_ref[2, m], taps_ref[3, m]) for m in range(23)]
     gap = iota((128, 128), 0) % 64 - iota((128, 128), 1) % 64 - 11
     gap = jnp.where(iota((128, 128), 0) // 64 == iota((128, 128), 1) // 64, gap, 99)
     hi, lo = split(banded(gap, ctap, 11))
@@ -480,7 +503,7 @@
             total = 0.0
             for g, weight in ((0, 1.0), (1, 0.5625), (-1, 0.5625), (3, -0.0625), (-3, -0.0625)):
                 if (d + g) % 2 == 0 and abs((d + g) // 2) <= 11:
-                    total = total + weight * ct[t, (d + g) // 2 + 11]
+                    total = total + weight * taps_ref[2 + t, (d + g) // 2 + 11]
             taps.append(total)
         cmy_m[40 * t : 40 * t + 40] = three_parts(40, 64, spots_cy, taps, 25)
     spot = iota((256, 128), 0) % 64 - 2
@@ -556,14 +579,14 @@
         v_ref[x] = near + far
 
 
-def field(fine_taps, coarse_taps, grid):
+def field(taps, grid):
     def scratch(*shape):
         return pltpu.VMEM(shape, f32)
 
     return pl.pallas_call(
         field_kernel,
         out_shape=jax.ShapeDtypeStruct((36, 40, 128), f32),
-        in_specs=[SMEM, SMEM, VMEM],
+        in_specs=[SMEM, VMEM],
         out_specs=VMEM,
         scratch_shapes=[
             scratch(2, 5, 40, 128),
@@ -597,24 +620,26 @@
             pltpu.SemaphoreType.DMA((7, 2)),
         ],
         compiler_params=pltpu.CompilerParams(
-            collective_id=0, has_side_effects=True, vmem_limit_bytes=48 * 1024 * 1024
+            collective_id=0, has_side_effects=True, vmem_limit_bytes=24 * 1024 * 1024
         ),
-    )(fine_taps, coarse_taps, grid)
+    )(taps, grid)
 
 
 def body(charge, positions, counts, corner, fine_taps, coarse_taps):
     ext_y = CY + 6
     ext_z = CZ + 6
-    cell_x = (corner // (ext_y * ext_z) - 2) // 4
-    cell_y = (corner // ext_z % ext_y - 2) // 4
-    cell_z = (corner % ext_z - 2) // 4
-    lattice = (cell_x * (CY // 4) + cell_y) * (CZ // 4) + cell_z
-    spots = jnp.arange(lattice.shape[0])
-    inv = jnp.sum(jnp.where(lattice[None, :] == spots[:, None], spots[None, :], 0), axis=1)
-    inv = inv.astype(jnp.int32)
-    grid = spread(inv, counts, charge, positions)
-    values = field(fine_taps, coarse_taps, grid)
-    return sample(inv, counts, positions, values)
+    count = corner.shape[0]
+    spots = np.arange(count, dtype=np.int32)
+    along_y, along_z = CY // 4, CZ // 4
+    cell_x, cell_y, cell_z = spots // (along_y * along_z), spots // along_z % along_y, spots % along_z
+    wanted = ((4 * cell_x + 2) * ext_y + 4 * cell_y + 2) * ext_z + 4 * cell_z + 2
+    same = corner[None, :] == wanted[:, None]
+    number = lax.broadcasted_iota(jnp.int32, (count, count), 1)
+    inv = jnp.sum(jnp.where(same, number, 0), axis=1, dtype=jnp.int32)
+    live = jnp.sum(jnp.where(same, counts[None, :], 0), axis=1, dtype=jnp.int32)
+    grid, planes, depths = spread(inv, live, charge, positions)
+    values = field(jnp.concatenate([fine_taps, coarse_taps], 0), grid)
+    return sample(inv, live, planes, depths, values)
 
 
 def solution(mesh):

time: 95.2 us -> 79.8 us (0.84)
  Pallas kernels: 89 us -> 73.1 us
  other arithmetic: 1.23 us -> 2.51 us
    pallas_call x1, Pallas kernels: 27 us -> 18.8 us  [spread(): pl.pallas_call(spread_kernel, out_shape=(jax.ShapeDtypeStruct((54, 40, 12...]
    pallas_call x1, Pallas kernels: 21.4 us -> 13.5 us  [sample(): pl.pallas_call(sample_kernel, out_shape=(jax.ShapeDtypeStruct((1024, 128)...]
    reduce_sum x1, other arithmetic: 0.5 us -> 1.81 us  [body(): live = jnp.sum(jnp.where(same, counts[None, :], 0), axis=1, dtype=jnp.int32)]
    unnamed x12 -> x4, local copies, waits for them, and re-layouts: 3.14 us -> 2.44 us
where the time goes in v1:
time: 79.8 us; the launch traced here: 78.7 us
  Pallas kernels  73.1 us (92%)
  other arithmetic  2.51 us (3%)
  local copies, waits for them, and re-layouts  2.44 us (3%)
    pallas_call x1, Pallas kernels, field(): pl.pallas_call(field_kernel, out_shape=jax.ShapeDtypeStruct((36, 40, 128)...  40.7 us
    pallas_call x1, Pallas kernels, spread(): pl.pallas_call(spread_kernel, out_shape=(jax.ShapeDtypeStruct((54, 40, 12...  18.8 us
    pallas_call x1, Pallas kernels, sample(): pl.pallas_call(sample_kernel, out_shape=(jax.ShapeDtypeStruct((1024, 128)...  13.5 us
    unnamed x4, local copies, waits for them, and re-layouts  2.44 us
    reduce_sum x1, other arithmetic, body(): live = jnp.sum(jnp.where(same, counts[None, :], 0), axis=1, dtype=jnp.int32)  1.81 us

profile of v1, /device:TPU:0, one launch (start us, length us, event | category | flops | bytes accessed | tf_op | source)
XLA Modules:
  0.0 78.7 jit_solution(14442729618807187853)
XLA Ops:
  0.6 0.7 pad_maximum_fusion.taps_ref
  1.3 1.8 %fusion.1 = (s32[1024]{0:T(1024)S(1)}, s32[1024]{0:T(1024)S(1)}) fusion(s32[1024]{0:T(1024)} %param.9, s32[1024]{0:T(1024)} %param.10, s32[1024]{0:T(1024)} %constant.5), kind=kLoop, calls=%fused_computation.3 | loop fusion | flops 5240832 | bytes 20480 | tf_op jit(solution)/shard_map/reduce_sum | solution.py:639
  3.1 0.0 copy-start
  3.2 1.4 %copy-done = f32[3,1024,128]{2,1,0:T(8,128)S(1)} copy-done((f32[3,1024,128]{2,1,0:T(8,128)S(1)}, f32[3,1024,128]{2,1,0:T(8,128)}, u32[]{:S(2)}) %copy-start) | copy-done | bytes 1572888
  4.6 0.0 copy-start.1
  4.6 1.0 %copy-done.1 = f32[1024,128]{1,0:T(8,128)S(1)} copy-done((f32[1024,128]{1,0:T(8,128)S(1)}, f32[1024,128]{1,0:T(8,128)}, u32[]{:S(2)}) %copy-start.1) | copy-done | bytes 524312
  5.6 18.8 %shard_map.86 = (f32[54,40,128]{2,1,0:T(8,128)S(1)}, f32[1024,2,8,128]{3,2,1,0:T(8,128)S(1)}, bf16[1024,2,16,128]{3,2,1,0:T(8,128)(2,1)S(1)}) custom-call(s32[1024]{0:T(1024)S(1)} %get-tuple-element.9.inv_ref, s32[1024]{0:T(1024)S(1)} %get-tuple-element.8.cnt_ref, f32[1024,128]{1,0:T(8,128)S(1)} %copy-done.1, f32[3,1024,128]{2,1,0:T(8,128)S(1)} %copy-done), custom_call_target="tpu_custom_call" | custom-call | tf_op jit(solution)/shard_map/pallas_call | solution.py:128
  24.4 40.7 %shard_map.87.v_ref = f32[36,40,128]{2,1,0:T(8,128)S(1)} custom-call(f32[4,23]{1,0:T(4,128)S(1)} %pad_maximum_fusion.taps_ref, f32[54,40,128]{2,1,0:T(8,128)S(1)} %get-tuple-element.7.q_ref), custom_call_target="tpu_custom_call" | custom-call | tf_op jit(solution)/shard_map/pallas_call | solution.py:586
  65.1 13.5 %shard_map.88 = (f32[1024,128]{1,0:T(8,128)}, f32[32,32,64]{2,1,0:T(8,128)}) custom-call(s32[1024]{0:T(1024)S(1)} %get-tuple-element.9.inv_ref, s32[1024]{0:T(1024)S(1)} %get-tuple-element.8.cnt_ref, f32[1024,2,8,128]{3,2,1,0:T(8,128)S(1)} %get-tuple-element.5.xy_ref, bf16[1024,2,16,128]{3,2,1,0:T(8,128)(2,1)S(1)} %get-tuple-element.6.z_ref, ...), custom_call_target="tpu_custom_call" | custom-call | tf_op jit(solution)/shard_map/pallas_call | solution.py:205
Async XLA Ops:
  3.1 1.4 %copy-start = (f32[3,1024,128]{2,1,0:T(8,128)S(1)}, f32[3,1024,128]{2,1,0:T(8,128)}, u32[]{:S(2)}) copy-start(f32[3,1024,128]{2,1,0:T(8,128)} %pos_ref.1) | copy-start | bytes 4718596
  4.6 1.0 %copy-start.1 = (f32[1024,128]{1,0:T(8,128)S(1)}, f32[1024,128]{1,0:T(8,128)}, u32[]{:S(2)}) copy-start(f32[1024,128]{1,0:T(8,128)} %q_ref.1) | copy-start | bytes 1572868

commit v2 on v1

--- a/solution.py
+++ b/solution.py
@@ -235,7 +235,7 @@
 def banded(gap, values, reach):
     total = jnp.zeros(gap.shape, f32)
     for m in range(-reach, reach + 1):
-        total = total + jnp.where(gap == m, values[m + reach], 0.0)
+        total = jnp.where(gap == m, values[m + reach], total)
     return total
 
 
@@ -250,11 +250,15 @@
     return jnp.dot(jnp.concatenate([hi, lo], 1), twice, preferred_element_type=f32)
 
 
+ORDER = (0, 4, 1, 3, 2)
+
+
 def field_kernel(
     taps_ref, q_ref, v_ref,
     zs, zr, a_ref, ys, yr, xr, ext, rs, rr,
     c_ref, cxs, cxr, cext, d_ref, czs, czr, e_ref, cys, cyr, g_ref,
-    cz_m, my_m, rz_m, ry_m, ccz_m, cmy_m, pz_m, ssem, rsem,
+    cz_m, my_m, rz_m, ry_m, ccz_m, cmy_m, pz_m,
+    zsem, ysem, xsem, csem, rsem,
 ):
     ids = {name: lax.axis_index(name) for name in ("gx", "gy", "gz")}
     size_of = {"gx": 4, "gy": 4, "gz": 8}
@@ -274,43 +278,34 @@
     lane = iota((1, 128), 1)
     lane40 = iota((40, 128), 1)
     lane24 = iota((24, 128), 1)
-    half40 = lane40 % 64
     half24 = lane24 % 64
 
-    def send(stage, name, up_src, up_dst, down_src, down_dst):
-        copies = []
-        for k, (step, src, dst) in enumerate(((1, up_src, up_dst), (-1, down_src, down_dst))):
-            copy = pltpu.make_async_remote_copy(
-                src_ref=src,
-                dst_ref=dst,
-                send_sem=ssem.at[stage, k],
-                recv_sem=rsem.at[stage, k],
-                device_id=away(name, step),
-                device_id_type=MESH,
-            )
-            copy.start()
-            copies.append(copy)
-        return copies
-
-    def finish(copies):
-        for copy in copies:
-            copy.wait()
-
-    def pack_z(g, carry):
+    def send(name, k, src, dst, sems, *spot):
+        copy = pltpu.make_async_remote_copy(
+            src_ref=src,
+            dst_ref=dst,
+            send_sem=sems.at[(0, *spot)],
+            recv_sem=sems.at[(1, *spot)],
+            device_id=away(name, 1 - 2 * k),
+            device_id_type=MESH,
+        )
+        copy.start()
+        return copy
+
+    z_copies = {}
+    for g in ORDER:
         up = jnp.zeros((40, 128), f32)
         down = jnp.zeros((40, 128), f32)
-        for i in range(8):
+        for i in range(8 if g < 4 else 4):
             v = q_ref[6 + 8 * g + i]
             here = lane40 // 16 == i
             up = jnp.where(here, pltpu.roll(v, (16 * i - 64) % 128, 1), up)
             down = jnp.where(here, pltpu.roll(v, (16 * i - 11) % 128, 1), down)
         zs[0, g] = up
         zs[1, g] = down
-        return carry
-
-    lax.fori_loop(0, 5, pack_z, 0)
-    pl.semaphore_wait(barrier, 6)
-    z_copies = send(0, "gz", zs.at[0], zr.at[0], zs.at[1], zr.at[1])
+        if g == 0:
+            pl.semaphore_wait(barrier, 6)
+        z_copies[g] = [send("gz", k, zs.at[k, g], zr.at[k, g], zsem, g, k) for k in range(2)]
 
     gap = iota((256, 128), 0) % 128 - 12 - 2 * (iota((256, 128), 1) % 64 - 13)
     node = iota((256, 128), 1) % 64 - 13
@@ -334,60 +329,58 @@
             c_ref[4 * g + i] = r[:, 128 * i : 128 * i + 128]
         return carry
 
-    lax.fori_loop(0, 6, shrink, 0)
+    lax.fori_loop(0, 6, shrink, 0, unroll=2)
     for k in range(8):
         cxs[0, k] = jnp.where(lane24 < 64, c_ref[5 + k], c_ref[13 + k])
         cxs[1, k] = jnp.where(lane24 < 64, c_ref[k], c_ref[8 + k])
-    cx_copies = send(1, "gx", cxs.at[0], cxr.at[0], cxs.at[1], cxr.at[1])
+    cx_copies = [send("gx", k, cxs.at[k], cxr.at[k], csem, 0, k) for k in range(2)]
 
     ftap = [jnp.where(lane < 64, taps_ref[0, m], taps_ref[1, m]) for m in range(23)]
     gap = iota((128, 128), 0) - 12 - iota((128, 128), 1) % 64
-    full = banded(gap, ftap, 11)
-    hi, lo = split(full)
+    hi, lo = split(banded(gap, ftap, 11))
     cz_m[0:128] = hi
     cz_m[128:256] = hi
     cz_m[256:384] = lo
-
-    def three_parts(rows, width, spots, values, reach):
-        col = iota((rows, 256), 1)
-        part = col // width
-        total = banded(spots(col % width), values, reach)
-        hi = total.astype(bf16).astype(f32)
-        return jnp.where(part == 2, total - hi, hi).astype(bf16)
-
-    row40 = iota((40, 256), 0)
-
-    def spots_y(col):
-        off = jnp.where(col < 40, col, jnp.where(col < 56, col - 52, col - 24))
-        return jnp.where(col < 72, off - row40, 99)
-
-    for t in range(2):
-        taps = [taps_ref[t, m] for m in range(23)]
-        my_m[40 * t : 40 * t + 40] = three_parts(40, 80, spots_y, taps, 11)
-
-    finish(z_copies)
-
-    def conv_z(g, carry):
+    row40 = iota((40, 128), 0)
+
+    def make_my():
+        off = jnp.where(lane40 < 40, lane40, jnp.where(lane40 < 56, lane40 - 52, lane40 - 24))
+        gap = jnp.where(lane40 < 72, off - row40, 99)
+        for t in range(2):
+            full = banded(gap, [taps_ref[t, m] for m in range(23)], 11)
+            hi = full.astype(bf16).astype(f32)
+            lo = full - hi
+            turned = pltpu.roll(hi, 80, 1)
+            first = jnp.where(lane40 < 80, hi, turned)
+            second = jnp.where(lane40 < 32, turned, pltpu.roll(lo, 32, 1))
+            my_m[40 * t : 40 * t + 40] = jnp.concatenate([first, second], 1).astype(bf16)
+
+    y_copies = {}
+    for n, g in enumerate(ORDER):
+        for copy in z_copies[g]:
+            copy.wait()
         up = zr[0, g]
         down = zr[1, g]
         rows = []
-        for i in range(8):
+        count = 8 if g < 4 else 4
+        for i in range(count):
             v = q_ref[6 + 8 * g + i]
             v = v + jnp.where(lane40 < 16, pltpu.roll(up, (-16 * i) % 128, 1), 0.0)
             here = (lane40 >= 75) & (lane40 < 91)
             v = v + jnp.where(here, pltpu.roll(down, (75 - 16 * i) % 128, 1), 0.0)
             rows.append(v)
         r = right(jnp.concatenate(rows, 0), cz_m[0:256], cz_m[256:384])
-        for i in range(8):
+        for i in range(count):
             part = r[40 * i : 40 * i + 40]
             a_ref[8 * g + i] = part
             ys[0, 8 * g + i] = part[20:36]
             ys[1, 8 * g + i] = part[0:16]
-        return carry
-
-    lax.fori_loop(0, 5, conv_z, 0)
-    own = pl.ds(0, 36)
-    y_copies = send(2, "gy", ys.at[0, own], yr.at[0, own], ys.at[1, own], yr.at[1, own])
+        own = pl.ds(8 * g, count)
+        y_copies[g] = [
+            send("gy", k, ys.at[k, own], yr.at[k, own], ysem, g, k) for k in range(2)
+        ]
+
+    make_my()
 
     ctap = [jnp.where(lane < 64, taps_ref[2, m], taps_ref[3, m]) for m in range(23)]
     gap = iota((128, 128), 0) % 64 - iota((128, 128), 1) % 64 - 11
@@ -396,11 +389,11 @@
     ccz_m[0:128] = hi
     ccz_m[128:256] = hi
     ccz_m[256:384] = lo
-    finish(cx_copies)
+    for copy in cx_copies:
+        copy.wait()
     for k in range(21):
         cext[11 + k] = c_ref[k]
     for s in range(2):
-        base = 0 if s == 0 else 27
         for k in range(8):
             v = cxr[s, k]
             w = pltpu.roll(v, 64, 1)
@@ -444,31 +437,38 @@
         czs[1, g] = down
         return carry
 
-    lax.fori_loop(0, 6, pack_cz, 0)
-    cz_copies = send(3, "gz", czs.at[0], czr.at[0], czs.at[1], czr.at[1])
-
-    finish(y_copies)
-
-    def conv_y(h, carry):
-        both = []
-        for p in range(2):
-            x = 2 * h + p
-            rows = [a_ref[x], yr[0, x], yr[1, x], jnp.zeros((8, 128), f32)]
-            both.append(jnp.concatenate(rows, 0))
-        hi, lo = split(jnp.concatenate(both, 1))
-        stack = jnp.concatenate([hi, lo, hi], 0)
-        r = jnp.dot(my_m[:, 0:240], stack, preferred_element_type=f32)
-        for p in range(2):
-            part = r[:, 128 * p : 128 * p + 128]
-            ext[11 + 2 * h + p] = jnp.where(lane40 < 64, part[0:40], part[40:80])
-        return carry
-
-    lax.fori_loop(0, 18, conv_y, 0, unroll=3)
-    x_copies = send(
-        4, "gx", ext.at[pl.ds(32, 15)], xr.at[0], ext.at[pl.ds(11, 15)], xr.at[1]
-    )
-
-    finish(cz_copies)
+    lax.fori_loop(0, 6, pack_cz, 0, unroll=2)
+    cz_copies = [send("gz", k, czs.at[k], czr.at[k], csem, 1, k) for k in range(2)]
+
+    pieces = {0: (1, 0, 8), 1: (1, 8, 15), 2: (0, 21, 24), 3: (0, 24, 32), 4: (0, 32, 36)}
+    x_copies = []
+
+    def conv_y(g):
+        for copy in y_copies[g]:
+            copy.wait()
+        for h in range(4 if g < 4 else 2):
+            both = []
+            for p in range(2):
+                x = 8 * g + 2 * h + p
+                rows = [a_ref[x], yr[0, x], yr[1, x], jnp.zeros((8, 128), f32)]
+                both.append(jnp.concatenate(rows, 0))
+            hi, lo = split(jnp.concatenate(both, 1))
+            stack = jnp.concatenate([hi, lo, hi], 0)
+            r = jnp.dot(my_m[:, 0:240], stack, preferred_element_type=f32)
+            for p in range(2):
+                part = r[:, 128 * p : 128 * p + 128]
+                ext[11 + 8 * g + 2 * h + p] = jnp.where(lane40 < 64, part[0:40], part[40:80])
+        k, low, high = pieces[g]
+        base = 0 if k else 21
+        src = ext.at[pl.ds(11 + low, high - low)]
+        dst = xr.at[k, pl.ds(low - base, high - low)]
+        x_copies.append(send("gx", k, src, dst, xsem, g))
+
+    conv_y(0)
+    conv_y(4)
+
+    for copy in cz_copies:
+        copy.wait()
 
     def conv_cz(g, carry):
         up = czr[0, g]
@@ -488,15 +488,16 @@
             cys[1, 4 * g + i] = part[0:16]
         return carry
 
-    lax.fori_loop(0, 6, conv_cz, 0)
+    lax.fori_loop(0, 6, conv_cz, 0, unroll=2)
+    conv_y(1)
+    conv_y(3)
+    conv_y(2)
     own = pl.ds(0, 21)
-    cy_copies = send(5, "gy", cys.at[0, own], cyr.at[0, own], cys.at[1, own], cyr.at[1, own])
-
-    def spots_cy(col):
-        spot = jnp.where(col < 24, col - 2, jnp.where(col < 40, col - 37, col - 26))
-        valid = ((col < 21) | (col >= 24)) & (col < 56)
-        return jnp.where(valid, 2 * spot - (row40 - 1), 99)
-
+    cy_copies = [send("gy", k, cys.at[k, own], cyr.at[k, own], csem, 2, k) for k in range(2)]
+
+    spot = jnp.where(lane40 < 24, lane40 - 2, jnp.where(lane40 < 40, lane40 - 37, lane40 - 26))
+    valid = ((lane40 < 21) | (lane40 >= 24)) & (lane40 < 56)
+    gap = jnp.where(valid, 2 * spot - (row40 - 1), 99)
     for t in range(2):
         taps = []
         for d in range(-25, 26):
@@ -505,14 +506,18 @@
                 if (d + g) % 2 == 0 and abs((d + g) // 2) <= 11:
                     total = total + weight * taps_ref[2 + t, (d + g) // 2 + 11]
             taps.append(total)
-        cmy_m[40 * t : 40 * t + 40] = three_parts(40, 64, spots_cy, taps, 25)
+        full = banded(gap, taps, 25)
+        hi = full.astype(bf16).astype(f32)
+        first = jnp.where(lane40 < 64, hi, pltpu.roll(hi, 64, 1))
+        cmy_m[40 * t : 40 * t + 40] = jnp.concatenate([first, full - hi], 1).astype(bf16)
     spot = iota((256, 128), 0) % 64 - 2
     point = iota((256, 128), 1)
     point = jnp.where(point == 127, -1, point)
     good = (spot <= 34) & (point <= 66)
     pz_m[...] = jnp.where(good, weight_of(point - 2 * spot), 0.0).astype(bf16)
 
-    finish(x_copies)
+    for copy in x_copies:
+        copy.wait()
     ext[0:11] = xr[0, 0:11]
     ext[11:15] += xr[0, 11:15]
     ext[43:47] += xr[1, 0:4]
@@ -540,9 +545,10 @@
             down = jnp.where(here, pltpu.roll(v, (4 * i) % 128, 1), down)
         rs[0, g] = up
         rs[1, g] = down
-    r_copies = send(6, "gz", rs.at[0], rr.at[0], rs.at[1], rr.at[1])
-
-    finish(cy_copies)
+    r_copies = [send("gz", k, rs.at[k], rr.at[k], rsem, k) for k in range(2)]
+
+    for copy in cy_copies:
+        copy.wait()
 
     def conv_cy(h, carry):
         both = []
@@ -562,21 +568,22 @@
         g_ref[2 * h + 1] = r[40:80]
         return carry
 
-    lax.fori_loop(0, 11, conv_cy, 0)
-    finish(r_copies)
+    lax.fori_loop(0, 11, conv_cy, 0, unroll=11)
     for x in range(36):
-        g, i = x // 32, x % 32
         h = x // 2
         if x % 2:
             far = g_ref[h + 2]
         else:
             far = 0.5625 * (g_ref[h + 1] + g_ref[h + 2]) - 0.0625 * (g_ref[h] + g_ref[h + 3])
-        near = jnp.where(lane40 < 64, v_ref[x], 0.0)
+        v_ref[x] = jnp.where(lane40 < 64, v_ref[x], 0.0) + far
+    for copy in r_copies:
+        copy.wait()
+    for x in range(36):
+        g, i = x // 32, x % 32
         above = pltpu.roll(rr[1, g], (64 - 4 * i) % 128, 1)
         below = pltpu.roll(rr[0, g], (124 - 4 * i) % 128, 1)
-        near = jnp.where((lane40 >= 64) & (lane40 < 67), above, near)
-        near = jnp.where(lane40 == 127, below, near)
-        v_ref[x] = near + far
+        rim = jnp.where((lane40 >= 64) & (lane40 < 67), above, 0.0)
+        v_ref[x] += jnp.where(lane40 == 127, below, rim)
 
 
 def field(taps, grid):
@@ -616,8 +623,11 @@
             pltpu.VMEM((384, 128), bf16),
             pltpu.VMEM((80, 256), bf16),
             pltpu.VMEM((256, 128), bf16),
-            pltpu.SemaphoreType.DMA((7, 2)),
-            pltpu.SemaphoreType.DMA((7, 2)),
+            pltpu.SemaphoreType.DMA((2, 5, 2)),
+            pltpu.SemaphoreType.DMA((2, 5, 2)),
+            pltpu.SemaphoreType.DMA((2, 5)),
+            pltpu.SemaphoreType.DMA((2, 3, 2)),
+            pltpu.SemaphoreType.DMA((2, 2)),
         ],
         compiler_params=pltpu.CompilerParams(
             collective_id=0, has_side_effects=True, vmem_limit_bytes=24 * 1024 * 1024

time: 79.8 us -> 77.5 us (0.971); the launches traced: 78.7 us -> 77.3 us
  Pallas kernels: 73.1 us -> 71.7 us
    pallas_call x1, Pallas kernels: 40.7 us -> 39.2 us  [field(): pl.pallas_call(field_kernel, out_shape=jax.ShapeDtypeStruct((36, 40, 128)...]
where the time goes in v2:
time: 77.5 us; the launch traced here: 77.3 us
  Pallas kernels  71.7 us (93%)
  other arithmetic  2.51 us (3%)
  local copies, waits for them, and re-layouts  2.44 us (3%)
    pallas_call x1, Pallas kernels, field(): pl.pallas_call(field_kernel, out_shape=jax.ShapeDtypeStruct((36, 40, 128)...  39.2 us
    pallas_call x1, Pallas kernels, spread(): pl.pallas_call(spread_kernel, out_shape=(jax.ShapeDtypeStruct((54, 40, 12...  18.8 us
    pallas_call x1, Pallas kernels, sample(): pl.pallas_call(sample_kernel, out_shape=(jax.ShapeDtypeStruct((1024, 128)...  13.6 us
    unnamed x4, local copies, waits for them, and re-layouts  2.44 us
    reduce_sum x1, other arithmetic, body(): live = jnp.sum(jnp.where(same, counts[None, :], 0), axis=1, dtype=jnp.int32)  1.81 us

profile of v2, /device:TPU:0, one launch (start us, length us, event | category | flops | bytes accessed | tf_op | source)
XLA Modules:
  0.0 77.3 jit_solution(1052581932917974331)
XLA Ops:
  0.6 0.7 pad_maximum_fusion.taps_ref
  1.3 1.8 %fusion.1 = (s32[1024]{0:T(1024)S(1)}, s32[1024]{0:T(1024)S(1)}) fusion(s32[1024]{0:T(1024)} %param.9, s32[1024]{0:T(1024)} %param.10, s32[1024]{0:T(1024)} %constant.5), kind=kLoop, calls=%fused_computation.3 | loop fusion | flops 5240832 | bytes 20480 | tf_op jit(solution)/shard_map/reduce_sum | solution.py:649
  3.1 0.0 copy-start
  3.2 1.4 %copy-done = f32[3,1024,128]{2,1,0:T(8,128)S(1)} copy-done((f32[3,1024,128]{2,1,0:T(8,128)S(1)}, f32[3,1024,128]{2,1,0:T(8,128)}, u32[]{:S(2)}) %copy-start) | copy-done | bytes 1572888
  4.6 0.0 copy-start.1
  4.6 1.0 %copy-done.1 = f32[1024,128]{1,0:T(8,128)S(1)} copy-done((f32[1024,128]{1,0:T(8,128)S(1)}, f32[1024,128]{1,0:T(8,128)}, u32[]{:S(2)}) %copy-start.1) | copy-done | bytes 524312
  5.6 18.8 %shard_map.86 = (f32[54,40,128]{2,1,0:T(8,128)S(1)}, f32[1024,2,8,128]{3,2,1,0:T(8,128)S(1)}, bf16[1024,2,16,128]{3,2,1,0:T(8,128)(2,1)S(1)}) custom-call(s32[1024]{0:T(1024)S(1)} %get-tuple-element.9.inv_ref, s32[1024]{0:T(1024)S(1)} %get-tuple-element.8.cnt_ref, f32[1024,128]{1,0:T(8,128)S(1)} %copy-done.1, f32[3,1024,128]{2,1,0:T(8,128)S(1)} %copy-done), custom_call_target="tpu_custom_call" | custom-call | tf_op jit(solution)/shard_map/pallas_call | solution.py:128
  24.4 39.2 %shard_map.87.v_ref = f32[36,40,128]{2,1,0:T(8,128)S(1)} custom-call(f32[4,23]{1,0:T(4,128)S(1)} %pad_maximum_fusion.taps_ref, f32[54,40,128]{2,1,0:T(8,128)S(1)} %get-tuple-element.7.q_ref), custom_call_target="tpu_custom_call" | custom-call | tf_op jit(solution)/shard_map/pallas_call | solution.py:593
  63.7 13.6 %shard_map.88 = (f32[1024,128]{1,0:T(8,128)}, f32[32,32,64]{2,1,0:T(8,128)}) custom-call(s32[1024]{0:T(1024)S(1)} %get-tuple-element.9.inv_ref, s32[1024]{0:T(1024)S(1)} %get-tuple-element.8.cnt_ref, f32[1024,2,8,128]{3,2,1,0:T(8,128)S(1)} %get-tuple-element.5.xy_ref, bf16[1024,2,16,128]{3,2,1,0:T(8,128)(2,1)S(1)} %get-tuple-element.6.z_ref, ...), custom_call_target="tpu_custom_call" | custom-call | tf_op jit(solution)/shard_map/pallas_call | solution.py:205
Async XLA Ops:
  3.1 1.4 %copy-start = (f32[3,1024,128]{2,1,0:T(8,128)S(1)}, f32[3,1024,128]{2,1,0:T(8,128)}, u32[]{:S(2)}) copy-start(f32[3,1024,128]{2,1,0:T(8,128)} %pos_ref.1) | copy-start | bytes 4718596
  4.6 1.0 %copy-start.1 = (f32[1024,128]{1,0:T(8,128)S(1)}, f32[1024,128]{1,0:T(8,128)}, u32[]{:S(2)}) copy-start(f32[1024,128]{1,0:T(8,128)} %q_ref.1) | copy-start | bytes 1572868

commit v3 on v2

--- a/solution.py
+++ b/solution.py
@@ -34,114 +34,8 @@
     return jnp.broadcast_to(ref[at, 0, a : a + 1, :], (8, 128))
 
 
-def spread_kernel(inv_ref, cnt_ref, q_ref, pos_ref, out_ref, xy_ref, z_ref, acc, place, qs, ts):
-    node = lax.broadcasted_iota(jnp.int32, (8, 128), 0).astype(f32) - 1.0
-    lane = lax.broadcasted_iota(jnp.int32, (8, 128), 1)
-    zero = jnp.zeros((8, 128), f32)
-    acc[...] = jnp.zeros_like(acc)
-    ts[...] = jnp.zeros_like(ts)
-
-    def cell(row, cz, spot):
-        at = row * 16 + cz
-        n = inv_ref[at]
-        q = jnp.where(lane < cnt_ref[at], row8(q_ref, None, n), 0.0)
-        wx = spline8(row8(pos_ref, 0, n), node)
-        wy = spline8(row8(pos_ref, 1, n), node)
-        wz = spline8(row8(pos_ref, 2, n), node)
-        xy_ref[at, 0] = wx
-        xy_ref[at, 1] = wy
-        qs[spot] = q * wx
-        prod = jnp.concatenate([row8(qs, spot, a) * wy for a in range(8)], axis=0)
-        tile = jnp.concatenate([zero, wz] if cz % 2 else [wz, zero], axis=0)
-        hi, lo = split(tile)
-        z_ref[at, 0] = hi
-        z_ref[at, 1] = lo
-        return split(prod), (hi, lo)
-
-    def line(odd, row):
-        parts = []
-        for half in range(2):
-            for k in range(4):
-                (ah, al), (bh, bl) = cell(row, 8 * half + 2 * k, 16 * odd + 8 * half + 2 * k)
-                (ch, cl), (dh, dl) = cell(row, 8 * half + 2 * k + 1, 16 * odd + 8 * half + 2 * k + 1)
-                left = jnp.concatenate(
-                    [jnp.concatenate([ah, ch], 1), jnp.concatenate([al, cl], 1)], 0
-                )
-                down = jnp.concatenate(
-                    [jnp.concatenate([bh, dh], 1), jnp.concatenate([bl, dl], 1)], 0
-                )
-                r = lax.dot_general(
-                    down, left, (((1,), (1,)), ((), ())), preferred_element_type=f32
-                )
-                parts.append(r[0:16] + r[16:32])
-        ts[odd] = jnp.concatenate(parts, 0)
-
-    def finish(i, odd):
-        spot = pl.ds(pl.multiple_of(i % 4 * 8, 8), 8)
-        t = ts[odd].T
-        t = t[0:64] + t[64:128]
-        for a in range(8):
-            acc[odd, 4 * (i // 4) + a, spot, :] += t[8 * a : 8 * a + 8]
-
-    def step(i, carry):
-        before = jnp.maximum(i - 1, 0)
-        finish(before, 0)
-        finish(before, 1)
-        line(0, 2 * i)
-        line(1, 2 * i + 1)
-        return carry
-
-    lax.fori_loop(0, 32, step, 0)
-    finish(31, 0)
-    finish(31, 1)
-
-    lin = lax.broadcasted_iota(jnp.int32, (256, 128), 0) % 128
-    z = 4 * (lin // 8) + lin % 8 + 11
-    place[...] = jnp.where(z == lax.broadcasted_iota(jnp.int32, (256, 128), 1), 1.0, 0.0).astype(bf16)
-    for x in range(6):
-        out_ref[x] = jnp.zeros((40, 128), f32)
-    for x in range(42, 54):
-        out_ref[x] = jnp.zeros((40, 128), f32)
-
-    def close(g, carry):
-        joined = []
-        for i in range(4):
-            x = 4 * g + i
-            pad = jnp.zeros((4, 128), f32)
-            even = jnp.concatenate([acc[0, x], pad, pad], 0)
-            odd = jnp.concatenate([pad, acc[1, x], pad], 0)
-            joined.append(even + odd)
-        hi, lo = split(jnp.concatenate(joined, 0))
-        r = jnp.dot(jnp.concatenate([hi, lo], 1), place[...], preferred_element_type=f32)
-        for i in range(4):
-            out_ref[6 + 4 * g + i] = r[40 * i : 40 * i + 40] * (1.0 / 216.0)
-        return carry
-
-    lax.fori_loop(0, 9, close, 0)
-
-
 SMEM = pl.BlockSpec(memory_space=pltpu.SMEM)
 VMEM = pl.BlockSpec(memory_space=pltpu.VMEM)
-
-
-def spread(inv, counts, charge, positions):
-    return pl.pallas_call(
-        spread_kernel,
-        out_shape=(
-            jax.ShapeDtypeStruct((54, 40, 128), f32),
-            jax.ShapeDtypeStruct((1024, 2, 8, 128), f32),
-            jax.ShapeDtypeStruct((1024, 2, 16, 128), bf16),
-        ),
-        in_specs=[SMEM, SMEM, VMEM, VMEM],
-        out_specs=(VMEM, VMEM, VMEM),
-        scratch_shapes=[
-            pltpu.VMEM((2, 36, 32, 128), f32),
-            pltpu.VMEM((256, 128), bf16),
-            pltpu.VMEM((32, 8, 128), f32),
-            pltpu.VMEM((2, 128, 128), f32),
-        ],
-        compiler_params=pltpu.CompilerParams(vmem_limit_bytes=28 * 1024 * 1024),
-    )(inv, counts, charge, positions)
 
 
 def sample_kernel(inv_ref, cnt_ref, xy_ref, z_ref, v_ref, out_ref, grid_ref, vs, place):
@@ -250,11 +144,9 @@
     return jnp.dot(jnp.concatenate([hi, lo], 1), twice, preferred_element_type=f32)
 
 
-ORDER = (0, 4, 1, 3, 2)
-
-
 def field_kernel(
-    taps_ref, q_ref, v_ref,
+    inv_ref, cnt_ref, taps_ref, charge_ref, pos_ref, v_ref, xy_ref, z_ref,
+    acc, place, qs, ts, q_ref,
     zs, zr, a_ref, ys, yr, xr, ext, rs, rr,
     c_ref, cxs, cxr, cext, d_ref, czs, czr, e_ref, cys, cyr, g_ref,
     cz_m, my_m, rz_m, ry_m, ccz_m, cmy_m, pz_m,
@@ -280,8 +172,8 @@
     lane24 = iota((24, 128), 1)
     half24 = lane24 % 64
 
-    def send(name, k, src, dst, sems, *spot):
-        copy = pltpu.make_async_remote_copy(
+    def link(name, k, src, dst, sems, *spot):
+        return pltpu.make_async_remote_copy(
             src_ref=src,
             dst_ref=dst,
             send_sem=sems.at[(0, *spot)],
@@ -289,23 +181,117 @@
             device_id=away(name, 1 - 2 * k),
             device_id_type=MESH,
         )
+
+    def send(*args):
+        copy = link(*args)
         copy.start()
         return copy
 
-    z_copies = {}
-    for g in ORDER:
+    def links_z(g):
+        return [link("gz", k, zs.at[k, g], zr.at[k, g], zsem, g, k) for k in range(2)]
+
+    def links_y(g):
+        own = pl.ds(8 * g, 8 if g < 4 else 4)
+        return [link("gy", k, ys.at[k, own], yr.at[k, own], ysem, g, k) for k in range(2)]
+
+    pieces = {0: (1, 0, 8), 1: (1, 8, 15), 2: (0, 21, 24), 3: (0, 24, 32), 4: (0, 32, 36)}
+
+    def link_x(g):
+        k, low, high = pieces[g]
+        base = 0 if k else 21
+        src = ext.at[pl.ds(11 + low, high - low)]
+        dst = xr.at[k, pl.ds(low - base, high - low)]
+        return link("gx", k, src, dst, xsem, g)
+
+    knot = iota((8, 128), 0).astype(f32) - 1.0
+    lane8 = iota((8, 128), 1)
+    zero = jnp.zeros((8, 128), f32)
+    acc[...] = jnp.zeros_like(acc)
+    ts[...] = jnp.zeros_like(ts)
+    for x in range(6):
+        q_ref[x] = jnp.zeros((40, 128), f32)
+    for x in range(42, 54):
+        q_ref[x] = jnp.zeros((40, 128), f32)
+
+    def cell(row, cz, spot):
+        at = row * 16 + cz
+        n = inv_ref[at]
+        q = jnp.where(lane8 < cnt_ref[at], row8(charge_ref, None, n), 0.0)
+        wx = spline8(row8(pos_ref, 0, n), knot)
+        wy = spline8(row8(pos_ref, 1, n), knot)
+        wz = spline8(row8(pos_ref, 2, n), knot)
+        xy_ref[at, 0] = wx
+        xy_ref[at, 1] = wy
+        qs[spot] = q * wx
+        prod = jnp.concatenate([row8(qs, spot, a) * wy for a in range(8)], axis=0)
+        tile = jnp.concatenate([zero, wz] if cz % 2 else [wz, zero], axis=0)
+        hi, lo = split(tile)
+        z_ref[at, 0] = hi
+        z_ref[at, 1] = lo
+        return split(prod), (hi, lo)
+
+    def line(odd, row):
+        parts = []
+        for k in range(8):
+            (ah, al), (bh, bl) = cell(row, 2 * k, 16 * odd + 2 * k)
+            (ch, cl), (dh, dl) = cell(row, 2 * k + 1, 16 * odd + 2 * k + 1)
+            left = jnp.concatenate(
+                [jnp.concatenate([ah, ch], 1), jnp.concatenate([al, cl], 1)], 0
+            )
+            down = jnp.concatenate(
+                [jnp.concatenate([bh, dh], 1), jnp.concatenate([bl, dl], 1)], 0
+            )
+            r = lax.dot_general(down, left, (((1,), (1,)), ((), ())), preferred_element_type=f32)
+            parts.append(r[0:16] + r[16:32])
+        ts[odd] = jnp.concatenate(parts, 0)
+
+    def slab_of(n):
+        late = jnp.minimum(n // 2, 1)
+        last = jnp.minimum(n // 5, 1)
+        return n + (late - last) * (9 - 2 * n) - 3 * last
+
+    def drain(i, odd):
+        spot = pl.ds(pl.multiple_of(i % 4 * 8, 8), 8)
+        t = ts[odd].T
+        t = t[0:64] + t[64:128]
+        for a in range(8):
+            acc[odd, 4 * slab_of(i // 4) + a, spot, :] += t[8 * a : 8 * a + 8]
+
+    def step(i, carry):
+        before = jnp.maximum(i - 1, 0)
+        drain(before, 0)
+        drain(before, 1)
+        row = 8 * slab_of(i // 4) + 2 * (i % 4)
+        line(0, row)
+        line(1, row + 1)
+        return carry
+
+    lin = iota((256, 128), 0) % 128
+    place[...] = jnp.where(4 * (lin // 8) + lin % 8 + 11 == iota((256, 128), 1), 1.0, 0.0).astype(bf16)
+
+    def close(g):
+        count = 8 if g < 4 else 4
+        joined = []
+        for i in range(count):
+            x = 8 * g + i
+            pad = jnp.zeros((4, 128), f32)
+            even = jnp.concatenate([acc[0, x], pad, pad], 0)
+            odd = jnp.concatenate([pad, acc[1, x], pad], 0)
+            joined.append(even + odd)
+        hi, lo = split(jnp.concatenate(joined, 0))
+        r = jnp.dot(jnp.concatenate([hi, lo], 1), place[...], preferred_element_type=f32)
         up = jnp.zeros((40, 128), f32)
         down = jnp.zeros((40, 128), f32)
-        for i in range(8 if g < 4 else 4):
-            v = q_ref[6 + 8 * g + i]
+        for i in range(count):
+            v = r[40 * i : 40 * i + 40] * (1.0 / 216.0)
+            q_ref[6 + 8 * g + i] = v
             here = lane40 // 16 == i
             up = jnp.where(here, pltpu.roll(v, (16 * i - 64) % 128, 1), up)
             down = jnp.where(here, pltpu.roll(v, (16 * i - 11) % 128, 1), down)
         zs[0, g] = up
         zs[1, g] = down
-        if g == 0:
-            pl.semaphore_wait(barrier, 6)
-        z_copies[g] = [send("gz", k, zs.at[k, g], zr.at[k, g], zsem, g, k) for k in range(2)]
+        for copy in links_z(g):
+            copy.start()
 
     gap = iota((256, 128), 0) % 128 - 12 - 2 * (iota((256, 128), 1) % 64 - 13)
     node = iota((256, 128), 1) % 64 - 13
@@ -329,12 +315,6 @@
             c_ref[4 * g + i] = r[:, 128 * i : 128 * i + 128]
         return carry
 
-    lax.fori_loop(0, 6, shrink, 0, unroll=2)
-    for k in range(8):
-        cxs[0, k] = jnp.where(lane24 < 64, c_ref[5 + k], c_ref[13 + k])
-        cxs[1, k] = jnp.where(lane24 < 64, c_ref[k], c_ref[8 + k])
-    cx_copies = [send("gx", k, cxs.at[k], cxr.at[k], csem, 0, k) for k in range(2)]
-
     ftap = [jnp.where(lane < 64, taps_ref[0, m], taps_ref[1, m]) for m in range(23)]
     gap = iota((128, 128), 0) - 12 - iota((128, 128), 1) % 64
     hi, lo = split(banded(gap, ftap, 11))
@@ -355,9 +335,10 @@
             second = jnp.where(lane40 < 32, turned, pltpu.roll(lo, 32, 1))
             my_m[40 * t : 40 * t + 40] = jnp.concatenate([first, second], 1).astype(bf16)
 
-    y_copies = {}
-    for n, g in enumerate(ORDER):
-        for copy in z_copies[g]:
+    make_my()
+
+    def conv_z(g):
+        for copy in links_z(g):
             copy.wait()
         up = zr[0, g]
         down = zr[1, g]
@@ -375,12 +356,84 @@
             a_ref[8 * g + i] = part
             ys[0, 8 * g + i] = part[20:36]
             ys[1, 8 * g + i] = part[0:16]
-        own = pl.ds(8 * g, count)
-        y_copies[g] = [
-            send("gy", k, ys.at[k, own], yr.at[k, own], ysem, g, k) for k in range(2)
-        ]
-
-    make_my()
+        for copy in links_y(g):
+            copy.start()
+
+    def conv_y(g):
+        for copy in links_y(g):
+            copy.wait()
+        for h in range(4 if g < 4 else 2):
+            both = []
+            for p in range(2):
+                x = 8 * g + 2 * h + p
+                rows = [a_ref[x], yr[0, x], yr[1, x], jnp.zeros((8, 128), f32)]
+                both.append(jnp.concatenate(rows, 0))
+            hi, lo = split(jnp.concatenate(both, 1))
+            stack = jnp.concatenate([hi, lo, hi], 0)
+            r = jnp.dot(my_m[:, 0:240], stack, preferred_element_type=f32)
+            for p in range(2):
+                part = r[:, 128 * p : 128 * p + 128]
+                ext[11 + 8 * g + 2 * h + p] = jnp.where(lane40 < 64, part[0:40], part[40:80])
+        link_x(g).start()
+    def flush(i):
+        for odd in range(2):
+            drain(i, odd)
+        ts[...] = jnp.zeros_like(ts)
+
+    lax.fori_loop(0, 8, step, 0)
+    flush(7)
+    pl.semaphore_wait(barrier, 6)
+    close(0)
+    shrink(0, 0)
+
+    def slab(n, carry):
+        lax.fori_loop(4 * n, 4 * n + 4, step, 0)
+
+        @pl.when(n == 2)
+        def _():
+            flush(11)
+            close(4)
+            shrink(5, 0)
+            conv_z(0)
+
+        @pl.when(n == 3)
+        def _():
+            conv_z(4)
+            conv_y(0)
+
+        @pl.when(n == 4)
+        def _():
+            flush(19)
+            close(3)
+            shrink(4, 0)
+            conv_y(4)
+
+        @pl.when(n == 5)
+        def _():
+            conv_z(3)
+
+        @pl.when(n == 6)
+        def _():
+            flush(27)
+            close(1)
+            shrink(1, 0)
+            conv_y(3)
+
+        return carry
+
+    lax.fori_loop(2, 8, slab, 0)
+    flush(31)
+    close(2)
+    shrink(2, 0)
+    shrink(3, 0)
+    for k in range(8):
+        cxs[0, k] = jnp.where(lane24 < 64, c_ref[5 + k], c_ref[13 + k])
+        cxs[1, k] = jnp.where(lane24 < 64, c_ref[k], c_ref[8 + k])
+    cx_copies = [send("gx", k, cxs.at[k], cxr.at[k], csem, 0, k) for k in range(2)]
+
+    conv_z(1)
+    conv_z(2)
+    conv_y(1)
 
     ctap = [jnp.where(lane < 64, taps_ref[2, m], taps_ref[3, m]) for m in range(23)]
     gap = iota((128, 128), 0) % 64 - iota((128, 128), 1) % 64 - 11
@@ -440,32 +493,7 @@
     lax.fori_loop(0, 6, pack_cz, 0, unroll=2)
     cz_copies = [send("gz", k, czs.at[k], czr.at[k], csem, 1, k) for k in range(2)]
 
-    pieces = {0: (1, 0, 8), 1: (1, 8, 15), 2: (0, 21, 24), 3: (0, 24, 32), 4: (0, 32, 36)}
-    x_copies = []
-
-    def conv_y(g):
-        for copy in y_copies[g]:
-            copy.wait()
-        for h in range(4 if g < 4 else 2):
-            both = []
-            for p in range(2):
-                x = 8 * g + 2 * h + p
-                rows = [a_ref[x], yr[0, x], yr[1, x], jnp.zeros((8, 128), f32)]
-                both.append(jnp.concatenate(rows, 0))
-            hi, lo = split(jnp.concatenate(both, 1))
-            stack = jnp.concatenate([hi, lo, hi], 0)
-            r = jnp.dot(my_m[:, 0:240], stack, preferred_element_type=f32)
-            for p in range(2):
-                part = r[:, 128 * p : 128 * p + 128]
-                ext[11 + 8 * g + 2 * h + p] = jnp.where(lane40 < 64, part[0:40], part[40:80])
-        k, low, high = pieces[g]
-        base = 0 if k else 21
-        src = ext.at[pl.ds(11 + low, high - low)]
-        dst = xr.at[k, pl.ds(low - base, high - low)]
-        x_copies.append(send("gx", k, src, dst, xsem, g))
-
-    conv_y(0)
-    conv_y(4)
+    conv_y(2)
 
     for copy in cz_copies:
         copy.wait()
@@ -489,9 +517,6 @@
         return carry
 
     lax.fori_loop(0, 6, conv_cz, 0, unroll=2)
-    conv_y(1)
-    conv_y(3)
-    conv_y(2)
     own = pl.ds(0, 21)
     cy_copies = [send("gy", k, cys.at[k, own], cyr.at[k, own], csem, 2, k) for k in range(2)]
 
@@ -516,16 +541,16 @@
     good = (spot <= 34) & (point <= 66)
     pz_m[...] = jnp.where(good, weight_of(point - 2 * spot), 0.0).astype(bf16)
 
-    for copy in x_copies:
-        copy.wait()
-    ext[0:11] = xr[0, 0:11]
+    for g in (0, 1, 3, 4):
+        link_x(g).wait()
+    ext[3:11] = xr[0, 3:11]
     ext[11:15] += xr[0, 11:15]
     ext[43:47] += xr[1, 0:4]
     ext[47:58] = xr[1, 4:15]
 
     def conv_x(k, carry):
-        rows = pl.ds(pl.multiple_of(8 * (k // 3), 8), 8)
-        first = 12 * lax.rem(k, 3)
+        rows = pl.ds(pl.multiple_of(8 * (k % 5), 8), 8)
+        first = 12 * (2 - k // 5)
         acc = ftap[0] * ext[pl.ds(first, 12), rows, :]
         for m in range(1, 23):
             acc = acc + ftap[m] * ext[pl.ds(first + m, 12), rows, :]
@@ -534,7 +559,10 @@
             v_ref[first + i, rows, :] = part + pltpu.roll(part, 64, 1)
         return carry
 
-    lax.fori_loop(0, 15, conv_x, 0)
+    lax.fori_loop(0, 10, conv_x, 0)
+    link_x(2).wait()
+    ext[0:3] = xr[0, 0:3]
+    lax.fori_loop(10, 15, conv_x, 0)
     for g in range(2):
         up = jnp.zeros((40, 128), f32)
         down = jnp.zeros((40, 128), f32)
@@ -586,16 +614,25 @@
         v_ref[x] += jnp.where(lane40 == 127, below, rim)
 
 
-def field(taps, grid):
+def field(inv, counts, taps, charge, positions):
     def scratch(*shape):
         return pltpu.VMEM(shape, f32)
 
     return pl.pallas_call(
         field_kernel,
-        out_shape=jax.ShapeDtypeStruct((36, 40, 128), f32),
-        in_specs=[SMEM, VMEM],
-        out_specs=VMEM,
+        out_shape=(
+            jax.ShapeDtypeStruct((36, 40, 128), f32),
+            jax.ShapeDtypeStruct((1024, 2, 8, 128), f32),
+            jax.ShapeDtypeStruct((1024, 2, 16, 128), bf16),
+        ),
+        in_specs=[SMEM, SMEM, SMEM, VMEM, VMEM],
+        out_specs=(VMEM, VMEM, VMEM),
         scratch_shapes=[
+            scratch(2, 36, 32, 128),
+            pltpu.VMEM((256, 128), bf16),
+            scratch(32, 8, 128),
+            scratch(2, 128, 128),
+            scratch(54, 40, 128),
             scratch(2, 5, 40, 128),
             scratch(2, 5, 40, 128),
             scratch(40, 40, 128),
@@ -630,9 +667,9 @@
             pltpu.SemaphoreType.DMA((2, 2)),
         ],
         compiler_params=pltpu.CompilerParams(
-            collective_id=0, has_side_effects=True, vmem_limit_bytes=24 * 1024 * 1024
+            collective_id=0, has_side_effects=True, vmem_limit_bytes=30 * 1024 * 1024
         ),
-    )(taps, grid)
+    )(inv, counts, taps, charge, positions)
 
 
 def body(charge, positions, counts, corner, fine_taps, coarse_taps):
@@ -647,8 +684,8 @@
     number = lax.broadcasted_iota(jnp.int32, (count, count), 1)
     inv = jnp.sum(jnp.where(same, number, 0), axis=1, dtype=jnp.int32)
     live = jnp.sum(jnp.where(same, counts[None, :], 0), axis=1, dtype=jnp.int32)
-    grid, planes, depths = spread(inv, live, charge, positions)
-    values = field(jnp.concatenate([fine_taps, coarse_taps], 0), grid)
+    taps = jnp.concatenate([fine_taps, coarse_taps], 0)
+    values, planes, depths = field(inv, live, taps, charge, positions)
     return sample(inv, live, planes, depths, values)
 
 

time: 77.5 us -> 72.1 us (0.930); the launches traced: 77.3 us -> 71 us
  Pallas kernels: 71.7 us -> 65.3 us
    pallas_call x2 -> x1, Pallas kernels: 58.1 us -> 51.8 us  [field(): pl.pallas_call(field_kernel, out_shape=(jax.ShapeDtypeStruct((36, 40, 128...]
where the time goes in v3:
time: 72.1 us; the launch traced here: 71 us
  Pallas kernels  65.3 us (91%)
  other arithmetic  2.51 us (3%)
  local copies, waits for them, and re-layouts  2.44 us (3%)
    pallas_call x1, Pallas kernels, field(): pl.pallas_call(field_kernel, out_shape=(jax.ShapeDtypeStruct((36, 40, 128...  51.8 us
    pallas_call x1, Pallas kernels, sample(): pl.pallas_call(sample_kernel, out_shape=(jax.ShapeDtypeStruct((1024, 128)...  13.6 us
    unnamed x4, local copies, waits for them, and re-layouts  2.44 us
    reduce_sum x1, other arithmetic, body(): live = jnp.sum(jnp.where(same, counts[None, :], 0), axis=1, dtype=jnp.int32)  1.81 us

profile of v3, /device:TPU:0, one launch (start us, length us, event | category | flops | bytes accessed | tf_op | source)
XLA Modules:
  0.0 71.0 jit_solution(11226400912037956229)
XLA Ops:
  0.6 0.7 pad_maximum_fusion.taps_ref
  1.3 1.8 %fusion.1 = (s32[1024]{0:T(1024)S(1)}, s32[1024]{0:T(1024)S(1)}) fusion(s32[1024]{0:T(1024)} %param.9, s32[1024]{0:T(1024)} %param.10, s32[1024]{0:T(1024)} %constant.5), kind=kLoop, calls=%fused_computation.3 | loop fusion | flops 5240832 | bytes 20480 | tf_op jit(solution)/shard_map/reduce_sum | solution.py:686
  3.1 0.0 copy-start
  3.2 1.4 %copy-done = f32[3,1024,128]{2,1,0:T(8,128)S(1)} copy-done((f32[3,1024,128]{2,1,0:T(8,128)S(1)}, f32[3,1024,128]{2,1,0:T(8,128)}, u32[]{:S(2)}) %copy-start) | copy-done | bytes 1572888
  4.6 0.0 copy-start.1
  4.6 1.0 %copy-done.1 = f32[1024,128]{1,0:T(8,128)S(1)} copy-done((f32[1024,128]{1,0:T(8,128)S(1)}, f32[1024,128]{1,0:T(8,128)}, u32[]{:S(2)}) %copy-start.1) | copy-done | bytes 524312
  5.6 51.8 %shard_map.86 = (f32[36,40,128]{2,1,0:T(8,128)S(1)}, f32[1024,2,8,128]{3,2,1,0:T(8,128)S(1)}, bf16[1024,2,16,128]{3,2,1,0:T(8,128)(2,1)S(1)}) custom-call(s32[1024]{0:T(1024)S(1)} %get-tuple-element.9.inv_ref, s32[1024]{0:T(1024)S(1)} %get-tuple-element.8.cnt_ref, f32[4,23]{1,0:T(4,128)S(1)} %pad_maximum_fusion.taps_ref, f32[1024,128]{1,0:T(8,128)S(1)} %copy-done.1, ...), custom_call_target="tpu_custom_call" | custom-call | tf_op jit(solution)/shard_map/pallas_call | solution.py:621
  57.4 13.6 %shard_map.87 = (f32[1024,128]{1,0:T(8,128)}, f32[32,32,64]{2,1,0:T(8,128)}) custom-call(s32[1024]{0:T(1024)S(1)} %get-tuple-element.9.inv_ref, s32[1024]{0:T(1024)S(1)} %get-tuple-element.8.cnt_ref, f32[1024,2,8,128]{3,2,1,0:T(8,128)S(1)} %get-tuple-element.5.xy_ref, bf16[1024,2,16,128]{3,2,1,0:T(8,128)(2,1)S(1)} %get-tuple-element.6.z_ref, ...), custom_call_target="tpu_custom_call" | custom-call | tf_op jit(solution)/shard_map/pallas_call | solution.py:99
Async XLA Ops:
  3.1 1.4 %copy-start = (f32[3,1024,128]{2,1,0:T(8,128)S(1)}, f32[3,1024,128]{2,1,0:T(8,128)}, u32[]{:S(2)}) copy-start(f32[3,1024,128]{2,1,0:T(8,128)} %pos_ref.1) | copy-start | bytes 4718596
  4.6 1.0 %copy-start.1 = (f32[1024,128]{1,0:T(8,128)S(1)}, f32[1024,128]{1,0:T(8,128)}, u32[]{:S(2)}) copy-start(f32[1024,128]{1,0:T(8,128)} %charge_ref.1) | copy-start | bytes 1572868

commit v4 on v3

--- a/solution.py
+++ b/solution.py
@@ -64,7 +64,7 @@
                     vs[1, k + p, 4 * g + i] = here[4:36]
         return carry
 
-    lax.fori_loop(0, 9, open_rows, 0)
+    lax.fori_loop(0, 9, open_rows, 0, unroll=3)
     for x in range(32):
         grid_ref[x] = v_ref[x + 1, 1:33, 0:64]
 
@@ -92,7 +92,7 @@
         one(cx, start, 1, 2 * i + 1)
         return carry
 
-    lax.fori_loop(0, 32, step, 0)
+    lax.fori_loop(0, 32, step, 0, unroll=4)
 
 
 def sample(inv, counts, planes, depths, grid):
@@ -380,44 +380,43 @@
             drain(i, odd)
         ts[...] = jnp.zeros_like(ts)
 
-    lax.fori_loop(0, 8, step, 0)
+    lax.fori_loop(0, 8, step, 0, unroll=2)
     flush(7)
     pl.semaphore_wait(barrier, 6)
     close(0)
     shrink(0, 0)
 
     def slab(n, carry):
-        lax.fori_loop(4 * n, 4 * n + 4, step, 0)
+        lax.fori_loop(0, 2, lambda m, c: step(4 * n + 2 * m + 1, step(4 * n + 2 * m, c)), 0)
 
         @pl.when(n == 2)
         def _():
             flush(11)
             close(4)
             shrink(5, 0)
-            conv_z(0)
 
         @pl.when(n == 3)
         def _():
-            conv_z(4)
-            conv_y(0)
+            conv_z(0)
 
         @pl.when(n == 4)
         def _():
             flush(19)
             close(3)
             shrink(4, 0)
-            conv_y(4)
+            conv_z(4)
 
         @pl.when(n == 5)
         def _():
-            conv_z(3)
+            conv_y(0)
 
         @pl.when(n == 6)
         def _():
             flush(27)
             close(1)
             shrink(1, 0)
-            conv_y(3)
+            conv_z(3)
+            conv_y(4)
 
         return carry
 
@@ -432,8 +431,8 @@
     cx_copies = [send("gx", k, cxs.at[k], cxr.at[k], csem, 0, k) for k in range(2)]
 
     conv_z(1)
+    conv_y(3)
     conv_z(2)
-    conv_y(1)
 
     ctap = [jnp.where(lane < 64, taps_ref[2, m], taps_ref[3, m]) for m in range(23)]
     gap = iota((128, 128), 0) % 64 - iota((128, 128), 1) % 64 - 11
@@ -493,6 +492,7 @@
     lax.fori_loop(0, 6, pack_cz, 0, unroll=2)
     cz_copies = [send("gz", k, czs.at[k], czr.at[k], csem, 1, k) for k in range(2)]
 
+    conv_y(1)
     conv_y(2)
 
     for copy in cz_copies:
@@ -680,10 +680,10 @@
     along_y, along_z = CY // 4, CZ // 4
     cell_x, cell_y, cell_z = spots // (along_y * along_z), spots // along_z % along_y, spots % along_z
     wanted = ((4 * cell_x + 2) * ext_y + 4 * cell_y + 2) * ext_z + 4 * cell_z + 2
-    same = corner[None, :] == wanted[:, None]
-    number = lax.broadcasted_iota(jnp.int32, (count, count), 1)
-    inv = jnp.sum(jnp.where(same, number, 0), axis=1, dtype=jnp.int32)
-    live = jnp.sum(jnp.where(same, counts[None, :], 0), axis=1, dtype=jnp.int32)
+    same = corner[:, None] == wanted[None, :]
+    number = lax.broadcasted_iota(jnp.int32, (count, count), 0)
+    inv = jnp.sum(jnp.where(same, number, 0), axis=0, dtype=jnp.int32)
+    live = jnp.sum(jnp.where(same, counts[:, None], 0), axis=0, dtype=jnp.int32)
     taps = jnp.concatenate([fine_taps, coarse_taps], 0)
     values, planes, depths = field(inv, live, taps, charge, positions)
     return sample(inv, live, planes, depths, values)

time: 72.1 us -> 61.8 us (0.86); the launches traced: 71 us -> 61.6 us
  Pallas kernels: 65.3 us -> 56.1 us
    pallas_call x1, Pallas kernels: 51.8 us -> 46.9 us  [field(): pl.pallas_call(field_kernel, out_shape=(jax.ShapeDtypeStruct((36, 40, 128...]
    pallas_call x1, Pallas kernels: 13.6 us -> 9.19 us  [sample(): pl.pallas_call(sample_kernel, out_shape=(jax.ShapeDtypeStruct((1024, 128)...]
where the time goes in v4:
time: 61.8 us; the launch traced here: 61.6 us
  Pallas kernels  56.1 us (91%)
  local copies, waits for them, and re-layouts  2.44 us (4%)
  other arithmetic  2.32 us (4%)
  between operations  0.66 us (1%)
    pallas_call x1, Pallas kernels, field(): pl.pallas_call(field_kernel, out_shape=(jax.ShapeDtypeStruct((36, 40, 128...  46.9 us
    pallas_call x1, Pallas kernels, sample(): pl.pallas_call(sample_kernel, out_shape=(jax.ShapeDtypeStruct((1024, 128)...  9.19 us
    unnamed x4, local copies, waits for them, and re-layouts  2.44 us
    reduce_sum x1, other arithmetic, body(): live = jnp.sum(jnp.where(same, counts[:, None], 0), axis=0, dtype=jnp.int32)  1.62 us

profile of v4, /device:TPU:0, one launch (start us, length us, event | category | flops | bytes accessed | tf_op | source)
XLA Modules:
  0.0 61.6 jit_solution(1215634953702371608)
XLA Ops:
  0.6 0.7 %pad_maximum_fusion.taps_ref = f32[4,23]{1,0:T(4,128)S(1)} fusion(f32[2,23]{1,0:T(2,128)} %param.12, f32[2,23]{1,0:T(2,128)} %param.11), kind=kLoop, calls=%fused_computation.4 | loop fusion | flops 92 | bytes 736 | tf_op jit(solution)/shard_map/concatenate | solution.py:687
  1.3 1.6 %fusion.1 = (s32[1024]{0:T(1024)S(1)}, s32[1024]{0:T(1024)S(1)}) fusion(s32[1024]{0:T(1024)} %param.9, s32[1024]{0:T(1024)} %constant.5, s32[1024]{0:T(1024)} %param.10), kind=kLoop, calls=%fused_computation.3 | loop fusion | flops 5240832 | bytes 20480 | tf_op jit(solution)/shard_map/reduce_sum | solution.py:686
  3.0 0.0 copy-start
  3.0 1.4 %copy-done = f32[3,1024,128]{2,1,0:T(8,128)S(1)} copy-done((f32[3,1024,128]{2,1,0:T(8,128)S(1)}, f32[3,1024,128]{2,1,0:T(8,128)}, u32[]{:S(2)}) %copy-start) | copy-done | bytes 1572888
  4.4 0.0 copy-start.1
  4.4 1.0 %copy-done.1 = f32[1024,128]{1,0:T(8,128)S(1)} copy-done((f32[1024,128]{1,0:T(8,128)S(1)}, f32[1024,128]{1,0:T(8,128)}, u32[]{:S(2)}) %copy-start.1) | copy-done | bytes 524312
  5.4 46.9 %shard_map.86 = (f32[36,40,128]{2,1,0:T(8,128)S(1)}, f32[1024,2,8,128]{3,2,1,0:T(8,128)S(1)}, bf16[1024,2,16,128]{3,2,1,0:T(8,128)(2,1)S(1)}) custom-call(s32[1024]{0:T(1024)S(1)} %get-tuple-element.9.inv_ref, s32[1024]{0:T(1024)S(1)} %get-tuple-element.8.cnt_ref, f32[4,23]{1,0:T(4,128)S(1)} %pad_maximum_fusion.taps_ref, f32[1024,128]{1,0:T(8,128)S(1)} %copy-done.1, ...), custom_call_target="tpu_custom_call" | custom-call | tf_op jit(solution)/shard_map/pallas_call | solution.py:621
  52.4 9.2 %shard_map.87 = (f32[1024,128]{1,0:T(8,128)}, f32[32,32,64]{2,1,0:T(8,128)}) custom-call(s32[1024]{0:T(1024)S(1)} %get-tuple-element.9.inv_ref, s32[1024]{0:T(1024)S(1)} %get-tuple-element.8.cnt_ref, f32[1024,2,8,128]{3,2,1,0:T(8,128)S(1)} %get-tuple-element.5.xy_ref, bf16[1024,2,16,128]{3,2,1,0:T(8,128)(2,1)S(1)} %get-tuple-element.6.z_ref, ...), custom_call_target="tpu_custom_call" | custom-call | tf_op jit(solution)/shard_map/pallas_call | solution.py:99
Async XLA Ops:
  3.0 1.4 %copy-start = (f32[3,1024,128]{2,1,0:T(8,128)S(1)}, f32[3,1024,128]{2,1,0:T(8,128)}, u32[]{:S(2)}) copy-start(f32[3,1024,128]{2,1,0:T(8,128)} %pos_ref.1) | copy-start | bytes 4718596
  4.4 1.0 %copy-start.1 = (f32[1024,128]{1,0:T(8,128)S(1)}, f32[1024,128]{1,0:T(8,128)}, u32[]{:S(2)}) copy-start(f32[1024,128]{1,0:T(8,128)} %charge_ref.1) | copy-start | bytes 1572868

commit v5 on v4

--- a/solution.py
+++ b/solution.py
@@ -92,7 +92,7 @@
         one(cx, start, 1, 2 * i + 1)
         return carry
 
-    lax.fori_loop(0, 32, step, 0, unroll=4)
+    lax.fori_loop(0, 32, step, 0, unroll=8)
 
 
 def sample(inv, counts, planes, depths, grid):
@@ -375,6 +375,16 @@
                 part = r[:, 128 * p : 128 * p + 128]
                 ext[11 + 8 * g + 2 * h + p] = jnp.where(lane40 < 64, part[0:40], part[40:80])
         link_x(g).start()
+    up_early = ((5, 16), (6, 17), (7, 18), (19, 20))
+
+    def links_cx(late):
+        copies = []
+        for k in range(2):
+            src = cxs.at[0 if late else k, pl.ds(4 * late, 4)]
+            dst = cxr.at[k, pl.ds(4 * late, 4)]
+            copies.append(link("gx", k, src, dst, csem, 3 * late, k))
+        return copies
+
     def flush(i):
         for odd in range(2):
             drain(i, odd)
@@ -387,7 +397,8 @@
     shrink(0, 0)
 
     def slab(n, carry):
-        lax.fori_loop(0, 2, lambda m, c: step(4 * n + 2 * m + 1, step(4 * n + 2 * m, c)), 0)
+        for r in range(4):
+            step(4 * n + r, 0)
 
         @pl.when(n == 2)
         def _():
@@ -415,6 +426,11 @@
             flush(27)
             close(1)
             shrink(1, 0)
+            for k, (first, second) in enumerate(up_early):
+                cxs[0, k] = jnp.where(lane24 < 64, c_ref[first], c_ref[second])
+                cxs[1, k] = jnp.where(lane24 < 64, c_ref[k], c_ref[4 + k])
+            for copy in links_cx(0):
+                copy.start()
             conv_z(3)
             conv_y(4)
 
@@ -425,10 +441,10 @@
     close(2)
     shrink(2, 0)
     shrink(3, 0)
-    for k in range(8):
-        cxs[0, k] = jnp.where(lane24 < 64, c_ref[5 + k], c_ref[13 + k])
-        cxs[1, k] = jnp.where(lane24 < 64, c_ref[k], c_ref[8 + k])
-    cx_copies = [send("gx", k, cxs.at[k], cxr.at[k], csem, 0, k) for k in range(2)]
+    for k in range(4):
+        cxs[0, 4 + k] = jnp.where(lane24 < 64, c_ref[8 + k], c_ref[12 + k])
+    for copy in links_cx(1):
+        copy.start()
 
     conv_z(1)
     conv_y(3)
@@ -441,28 +457,29 @@
     ccz_m[0:128] = hi
     ccz_m[128:256] = hi
     ccz_m[256:384] = lo
-    for copy in cx_copies:
+    conv_y(1)
+    for copy in links_cx(0) + links_cx(1):
         copy.wait()
     for k in range(21):
         cext[11 + k] = c_ref[k]
-    for s in range(2):
-        for k in range(8):
-            v = cxr[s, k]
+
+    def put(spot, v):
+        if 11 <= spot < 32:
+            cext[spot] += v
+        else:
+            cext[spot] = v
+
+    for k in range(2):
+        for i in range(8):
+            v = cxr[k, i]
             w = pltpu.roll(v, 64, 1)
-            first = jnp.where(lane24 < 64, v, w)
-            second = jnp.where(lane24 < 64, w, v)
-            if s == 0:
-                cext[k] = first
-                if 8 + k >= 11:
-                    cext[8 + k] += second
-                else:
-                    cext[8 + k] = second
+            if i >= 4:
+                pair = (4 + i, 8 + i)
             else:
-                if 27 + k < 32:
-                    cext[27 + k] += first
-                else:
-                    cext[27 + k] = first
-                cext[35 + k] = second
+                pair = (i, 4 + i) if k else up_early[i]
+            base = 27 if k else -5
+            put(base + pair[0], jnp.where(lane24 < 64, v, w))
+            put(base + pair[1], jnp.where(lane24 < 64, w, v))
 
     def conv_cx(c, carry):
         rows = pl.ds(pl.multiple_of(8 * c, 8), 8)
@@ -492,7 +509,6 @@
     lax.fori_loop(0, 6, pack_cz, 0, unroll=2)
     cz_copies = [send("gz", k, czs.at[k], czr.at[k], csem, 1, k) for k in range(2)]
 
-    conv_y(1)
     conv_y(2)
 
     for copy in cz_copies:
@@ -559,21 +575,23 @@
             v_ref[first + i, rows, :] = part + pltpu.roll(part, 64, 1)
         return carry
 
-    lax.fori_loop(0, 10, conv_x, 0)
-    link_x(2).wait()
-    ext[0:3] = xr[0, 0:3]
-    lax.fori_loop(10, 15, conv_x, 0)
-    for g in range(2):
+    r_copies = []
+    for g in (2, 1, 0):
+        if g == 0:
+            link_x(2).wait()
+            ext[0:3] = xr[0, 0:3]
+        lax.fori_loop(10 - 5 * g, 15 - 5 * g, conv_x, 0)
         up = jnp.zeros((40, 128), f32)
         down = jnp.zeros((40, 128), f32)
-        for i in range(32 if g == 0 else 4):
-            v = v_ref[32 * g + i]
+        for i in range(12):
+            v = v_ref[12 * g + i]
             here = lane40 // 4 == i
             up = jnp.where(here, pltpu.roll(v, (4 * i - 60) % 128, 1), up)
             down = jnp.where(here, pltpu.roll(v, (4 * i) % 128, 1), down)
         rs[0, g] = up
         rs[1, g] = down
-    r_copies = [send("gz", k, rs.at[k], rr.at[k], rsem, k) for k in range(2)]
+        for k in range(2):
+            r_copies.append(send("gz", k, rs.at[k, g], rr.at[k, g], rsem, g, k))
 
     for copy in cy_copies:
         copy.wait()
@@ -607,7 +625,7 @@
     for copy in r_copies:
         copy.wait()
     for x in range(36):
-        g, i = x // 32, x % 32
+        g, i = x // 12, x % 12
         above = pltpu.roll(rr[1, g], (64 - 4 * i) % 128, 1)
         below = pltpu.roll(rr[0, g], (124 - 4 * i) % 128, 1)
         rim = jnp.where((lane40 >= 64) & (lane40 < 67), above, 0.0)
@@ -640,8 +658,8 @@
             scratch(2, 40, 16, 128),
             scratch(2, 15, 40, 128),
             scratch(58, 40, 128),
-            scratch(2, 2, 40, 128),
-            scratch(2, 2, 40, 128),
+            scratch(2, 3, 40, 128),
+            scratch(2, 3, 40, 128),
             scratch(24, 24, 128),
             scratch(2, 8, 24, 128),
             scratch(2, 8, 24, 128),
@@ -663,8 +681,8 @@
             pltpu.SemaphoreType.DMA((2, 5, 2)),
             pltpu.SemaphoreType.DMA((2, 5, 2)),
             pltpu.SemaphoreType.DMA((2, 5)),
+            pltpu.SemaphoreType.DMA((2, 4, 2)),
             pltpu.SemaphoreType.DMA((2, 3, 2)),
-            pltpu.SemaphoreType.DMA((2, 2)),
         ],
         compiler_params=pltpu.CompilerParams(
             collective_id=0, has_side_effects=True, vmem_limit_bytes=30 * 1024 * 1024

time: 61.8 us -> 59.7 us (0.966)
  Pallas kernels: 56.1 us -> 54 us
    pallas_call x1, Pallas kernels: 46.9 us -> 45.4 us  [field(): pl.pallas_call(field_kernel, out_shape=(jax.ShapeDtypeStruct((36, 40, 128...]
where the time goes in v5:
time: 59.7 us; the launch traced here: 59.4 us
  Pallas kernels  54 us (90%)
  local copies, waits for them, and re-layouts  2.44 us (4%)
  other arithmetic  2.32 us (4%)
  between operations  0.66 us (1%)
    pallas_call x1, Pallas kernels, field(): pl.pallas_call(field_kernel, out_shape=(jax.ShapeDtypeStruct((36, 40, 128...  45.4 us
    pallas_call x1, Pallas kernels, sample(): pl.pallas_call(sample_kernel, out_shape=(jax.ShapeDtypeStruct((1024, 128)...  8.66 us
    unnamed x4, local copies, waits for them, and re-layouts  2.44 us
    reduce_sum x1, other arithmetic, body(): live = jnp.sum(jnp.where(same, counts[:, None], 0), axis=0, dtype=jnp.int32)  1.62 us

profile of v5, /device:TPU:0, one launch (start us, length us, event | category | flops | bytes accessed | tf_op | source)
XLA Modules:
  0.0 59.4 jit_solution(15220645181855571106)
XLA Ops:
  0.6 0.7 %pad_maximum_fusion.taps_ref = f32[4,23]{1,0:T(4,128)S(1)} fusion(f32[2,23]{1,0:T(2,128)} %param.12, f32[2,23]{1,0:T(2,128)} %param.11), kind=kLoop, calls=%fused_computation.4 | loop fusion | flops 92 | bytes 736 | tf_op jit(solution)/shard_map/concatenate | solution.py:705
  1.3 1.6 %fusion.1 = (s32[1024]{0:T(1024)S(1)}, s32[1024]{0:T(1024)S(1)}) fusion(s32[1024]{0:T(1024)} %param.9, s32[1024]{0:T(1024)} %constant.5, s32[1024]{0:T(1024)} %param.10), kind=kLoop, calls=%fused_computation.3 | loop fusion | flops 5240832 | bytes 20480 | tf_op jit(solution)/shard_map/reduce_sum | solution.py:704
  3.0 0.0 copy-start
  3.0 1.4 %copy-done = f32[3,1024,128]{2,1,0:T(8,128)S(1)} copy-done((f32[3,1024,128]{2,1,0:T(8,128)S(1)}, f32[3,1024,128]{2,1,0:T(8,128)}, u32[]{:S(2)}) %copy-start) | copy-done | bytes 1572888
  4.4 0.0 copy-start.1
  4.4 1.0 %copy-done.1 = f32[1024,128]{1,0:T(8,128)S(1)} copy-done((f32[1024,128]{1,0:T(8,128)S(1)}, f32[1024,128]{1,0:T(8,128)}, u32[]{:S(2)}) %copy-start.1) | copy-done | bytes 524312
  5.4 45.4 %shard_map.86 = (f32[36,40,128]{2,1,0:T(8,128)S(1)}, f32[1024,2,8,128]{3,2,1,0:T(8,128)S(1)}, bf16[1024,2,16,128]{3,2,1,0:T(8,128)(2,1)S(1)}) custom-call(s32[1024]{0:T(1024)S(1)} %get-tuple-element.9.inv_ref, s32[1024]{0:T(1024)S(1)} %get-tuple-element.8.cnt_ref, f32[4,23]{1,0:T(4,128)S(1)} %pad_maximum_fusion.taps_ref, f32[1024,128]{1,0:T(8,128)S(1)} %copy-done.1, ...), custom_call_target="tpu_custom_call" | custom-call | tf_op jit(solution)/shard_map/pallas_call | solution.py:639
  50.8 8.7 %shard_map.87 = (f32[1024,128]{1,0:T(8,128)}, f32[32,32,64]{2,1,0:T(8,128)}) custom-call(s32[1024]{0:T(1024)S(1)} %get-tuple-element.9.inv_ref, s32[1024]{0:T(1024)S(1)} %get-tuple-element.8.cnt_ref, f32[1024,2,8,128]{3,2,1,0:T(8,128)S(1)} %get-tuple-element.5.xy_ref, bf16[1024,2,16,128]{3,2,1,0:T(8,128)(2,1)S(1)} %get-tuple-element.6.z_ref, ...), custom_call_target="tpu_custom_call" | custom-call | tf_op jit(solution)/shard_map/pallas_call | solution.py:99
Async XLA Ops:
  3.0 1.4 %copy-start = (f32[3,1024,128]{2,1,0:T(8,128)S(1)}, f32[3,1024,128]{2,1,0:T(8,128)}, u32[]{:S(2)}) copy-start(f32[3,1024,128]{2,1,0:T(8,128)} %pos_ref.1) | copy-start | bytes 4718596
  4.4 1.0 %copy-start.1 = (f32[1024,128]{1,0:T(8,128)S(1)}, f32[1024,128]{1,0:T(8,128)}, u32[]{:S(2)}) copy-start(f32[1024,128]{1,0:T(8,128)} %charge_ref.1) | copy-start | bytes 1572868

commit v6 on v5

--- a/solution.py
+++ b/solution.py
@@ -64,7 +64,7 @@
                     vs[1, k + p, 4 * g + i] = here[4:36]
         return carry
 
-    lax.fori_loop(0, 9, open_rows, 0, unroll=3)
+    lax.fori_loop(0, 9, open_rows, 0, unroll=9)
     for x in range(32):
         grid_ref[x] = v_ref[x + 1, 1:33, 0:64]
 
@@ -92,7 +92,7 @@
         one(cx, start, 1, 2 * i + 1)
         return carry
 
-    lax.fori_loop(0, 32, step, 0, unroll=8)
+    lax.fori_loop(0, 32, step, 0, unroll=16)
 
 
 def sample(inv, counts, planes, depths, grid):
@@ -390,7 +390,7 @@
             drain(i, odd)
         ts[...] = jnp.zeros_like(ts)
 
-    lax.fori_loop(0, 8, step, 0, unroll=2)
+    lax.fori_loop(0, 8, step, 0, unroll=4)
     flush(7)
     pl.semaphore_wait(barrier, 6)
     close(0)
@@ -490,7 +490,7 @@
             d_ref[first : first + 7, rows, :] = acc
         return carry
 
-    lax.fori_loop(0, 3, conv_cx, 0)
+    lax.fori_loop(0, 3, conv_cx, 0, unroll=3)
     for j in range(21, 24):
         d_ref[j] = jnp.zeros((24, 128), f32)
 
@@ -506,7 +506,7 @@
         czs[1, g] = down
         return carry
 
-    lax.fori_loop(0, 6, pack_cz, 0, unroll=2)
+    lax.fori_loop(0, 6, pack_cz, 0, unroll=6)
     cz_copies = [send("gz", k, czs.at[k], czr.at[k], csem, 1, k) for k in range(2)]
 
     conv_y(2)
@@ -532,7 +532,7 @@
             cys[1, 4 * g + i] = part[0:16]
         return carry
 
-    lax.fori_loop(0, 6, conv_cz, 0, unroll=2)
+    lax.fori_loop(0, 6, conv_cz, 0, unroll=6)
     own = pl.ds(0, 21)
     cy_copies = [send("gy", k, cys.at[k, own], cyr.at[k, own], csem, 2, k) for k in range(2)]
 
@@ -580,7 +580,7 @@
         if g == 0:
             link_x(2).wait()
             ext[0:3] = xr[0, 0:3]
-        lax.fori_loop(10 - 5 * g, 15 - 5 * g, conv_x, 0)
+        lax.fori_loop(10 - 5 * g, 15 - 5 * g, conv_x, 0, unroll=5)
         up = jnp.zeros((40, 128), f32)
         down = jnp.zeros((40, 128), f32)
         for i in range(12):

time: 59.7 us -> 57.3 us (0.960)
  Pallas kernels: 54 us -> 51.6 us
    pallas_call x1, Pallas kernels: 45.4 us -> 43.7 us  [field(): pl.pallas_call(field_kernel, out_shape=(jax.ShapeDtypeStruct((36, 40, 128...]
    pallas_call x1, Pallas kernels: 8.66 us -> 7.96 us  [sample(): pl.pallas_call(sample_kernel, out_shape=(jax.ShapeDtypeStruct((1024, 128)...]
where the time goes in v6:
time: 57.3 us; the launch traced here: 57.1 us
  Pallas kernels  51.6 us (90%)
  local copies, waits for them, and re-layouts  2.44 us (4%)
  other arithmetic  2.32 us (4%)
  between operations  0.66 us (1%)
    pallas_call x1, Pallas kernels, field(): pl.pallas_call(field_kernel, out_shape=(jax.ShapeDtypeStruct((36, 40, 128...  43.7 us
    pallas_call x1, Pallas kernels, sample(): pl.pallas_call(sample_kernel, out_shape=(jax.ShapeDtypeStruct((1024, 128)...  7.96 us
    unnamed x4, local copies, waits for them, and re-layouts  2.44 us
    reduce_sum x1, other arithmetic, body(): live = jnp.sum(jnp.where(same, counts[:, None], 0), axis=0, dtype=jnp.int32)  1.62 us

profile of v6, /device:TPU:0, one launch (start us, length us, event | category | flops | bytes accessed | tf_op | source)
XLA Modules:
  0.0 57.1 jit_solution(17620296012385809153)
XLA Ops:
  0.6 0.7 %pad_maximum_fusion.taps_ref = f32[4,23]{1,0:T(4,128)S(1)} fusion(f32[2,23]{1,0:T(2,128)} %param.12, f32[2,23]{1,0:T(2,128)} %param.11), kind=kLoop, calls=%fused_computation.4 | loop fusion | flops 92 | bytes 736 | tf_op jit(solution)/shard_map/concatenate | solution.py:705
  1.3 1.6 %fusion.1 = (s32[1024]{0:T(1024)S(1)}, s32[1024]{0:T(1024)S(1)}) fusion(s32[1024]{0:T(1024)} %param.9, s32[1024]{0:T(1024)} %constant.5, s32[1024]{0:T(1024)} %param.10), kind=kLoop, calls=%fused_computation.3 | loop fusion | flops 5240832 | bytes 20480 | tf_op jit(solution)/shard_map/reduce_sum | solution.py:704
  3.0 0.0 copy-start
  3.0 1.4 %copy-done = f32[3,1024,128]{2,1,0:T(8,128)S(1)} copy-done((f32[3,1024,128]{2,1,0:T(8,128)S(1)}, f32[3,1024,128]{2,1,0:T(8,128)}, u32[]{:S(2)}) %copy-start) | copy-done | bytes 1572888
  4.4 0.0 copy-start.1
  4.4 1.0 %copy-done.1 = f32[1024,128]{1,0:T(8,128)S(1)} copy-done((f32[1024,128]{1,0:T(8,128)S(1)}, f32[1024,128]{1,0:T(8,128)}, u32[]{:S(2)}) %copy-start.1) | copy-done | bytes 524312
  5.4 43.7 %shard_map.86 = (f32[36,40,128]{2,1,0:T(8,128)S(1)}, f32[1024,2,8,128]{3,2,1,0:T(8,128)S(1)}, bf16[1024,2,16,128]{3,2,1,0:T(8,128)(2,1)S(1)}) custom-call(s32[1024]{0:T(1024)S(1)} %get-tuple-element.9.inv_ref, s32[1024]{0:T(1024)S(1)} %get-tuple-element.8.cnt_ref, f32[4,23]{1,0:T(4,128)S(1)} %pad_maximum_fusion.taps_ref, f32[1024,128]{1,0:T(8,128)S(1)} %copy-done.1, ...), custom_call_target="tpu_custom_call" | custom-call | tf_op jit(solution)/shard_map/pallas_call | solution.py:639
  49.1 8.0 %shard_map.87 = (f32[1024,128]{1,0:T(8,128)}, f32[32,32,64]{2,1,0:T(8,128)}) custom-call(s32[1024]{0:T(1024)S(1)} %get-tuple-element.9.inv_ref, s32[1024]{0:T(1024)S(1)} %get-tuple-element.8.cnt_ref, f32[1024,2,8,128]{3,2,1,0:T(8,128)S(1)} %get-tuple-element.5.xy_ref, bf16[1024,2,16,128]{3,2,1,0:T(8,128)(2,1)S(1)} %get-tuple-element.6.z_ref, ...), custom_call_target="tpu_custom_call" | custom-call | tf_op jit(solution)/shard_map/pallas_call | solution.py:99
Async XLA Ops:
  3.0 1.4 %copy-start = (f32[3,1024,128]{2,1,0:T(8,128)S(1)}, f32[3,1024,128]{2,1,0:T(8,128)}, u32[]{:S(2)}) copy-start(f32[3,1024,128]{2,1,0:T(8,128)} %pos_ref.1) | copy-start | bytes 4718596
  4.4 1.0 %copy-start.1 = (f32[1024,128]{1,0:T(8,128)S(1)}, f32[1024,128]{1,0:T(8,128)}, u32[]{:S(2)}) copy-start(f32[1024,128]{1,0:T(8,128)} %charge_ref.1) | copy-start | bytes 1572868
